TPU v7x, 256 devices: a whole 4x4x8 slice. The times are simulated.
256 devices in a mesh: gx: 8 (over z), gy: 8 (over y, core), gz: 4 (over x).
Axes of the slice: x: 4, y: 4, z: 8, core: 2. Of those that a mesh axis runs over, the one named last changes fastest.
Arguments:
- adjoint_disp: float32 [3, 32, 64, 512], P(None, 'gx', 'gy', 'gz'), may hold values from -6 to 6
- matrix_tangent: float32 [6, 6], replicated, may hold values from -6 to 6
- fibre_blocks: bfloat16 [36, 512], replicated, may hold values from -24 to 24
- fibre_weights: bfloat16 [1048576, 512], P(('gx', 'gy', 'gz')), may hold values from 0.099609375 to 10
- rve_class: int32 [1048576], P(('gx', 'gy', 'gz')), may hold values from 0 to 3
- rve_helper: int32 [32, 64, 512], P('gx', 'gy', 'gz'), may hold values from 0 to 63, as said below
- rve_slot: int32 [32, 64, 512], P('gx', 'gy', 'gz'), may hold values from 0 to 4095, as said below
Outputs:
- node_force: float32 [3, 32, 64, 512], P(None, 'gx', 'gy', 'gz')
Inputs may be any that keep to these rules, and one draw needn't show every extreme that they name: `rve_helper`: positions count along gx and gy with gx first. The number of points that one device sends to the owner k positions after its own (mod 64) depends only on k, is at most 128, and equals 128 for some k. `rve_slot`: for each owner and each gz plane, the points of that plane whose RVE lies with that owner name each of its 4096 rows exactly once.
All inputs are finite; a program needn't handle non-finite values.
Results may differ from a plain program's by a relative error of at most 0.0003.
Values sent between devices are 32-bit elements; how exact they have to be, the bound alone decides.
No kernel may reach another device: no remote copies, remote signals or barrier semaphores. Data moves between devices by JAX's collectives and lax.ppermute only.
A program may use at most 64 MiB of HBM per device.

v0:
```python
import math

import jax
import jax.numpy as jnp
from jax import lax
from jax.sharding import PartitionSpec as P

CLASSES = 4


SIGNS = (-0.25, 0.25)


def passed_along(array, axis, by):
    devices = lax.axis_size(axis)
    pairs = [(i, i + by) for i in range(devices) if 0 <= i + by < devices]
    return lax.ppermute(array, axis, pairs)


def lift(field):
    upper_x = passed_along(field[:, :1], "gx", -1)
    section_x = jnp.stack([field, jnp.concatenate([field[:, 1:], upper_x], 1)])
    upper_y = passed_along(section_x[:, :, :, :1], "gy", -1)
    section_y = jnp.stack([section_x, jnp.concatenate([section_x[:, :, :, 1:], upper_y], 3)], 1)
    upper_z = passed_along(section_y[..., :1], "gz", -1)
    return jnp.stack([section_y, jnp.concatenate([section_y[..., 1:], upper_z], 5)], 2)


def settle(pieces):
    lower_z = passed_along(pieces[:, :, 1, ..., -1:], "gz", 1)
    sheet = pieces[:, :, 0] + jnp.concatenate([lower_z, pieces[:, :, 1, ..., :-1]], 5)
    lower_y = passed_along(sheet[:, 1, :, :, -1:], "gy", 1)
    strip = sheet[:, 0] + jnp.concatenate([lower_y, sheet[:, 1, :, :, :-1]], 3)
    lower_x = passed_along(strip[1, :, -1:], "gx", 1)
    return strip[0] + jnp.concatenate([lower_x, strip[1, :, :-1]], 1)


def respond(tangent_rows, arrived, asked):
    owners, items = (asked.shape[0], asked.shape[2])
    picked = jnp.take(tangent_rows, asked.reshape(-1), axis=0).reshape(owners, items, 6, 6)
    return jnp.einsum("hnij,hin->hjn", picked, arrived, precision=lax.Precision.HIGHEST)


def ranks_within(helper_flat, owners, points):
    block = math.gcd(points, 128)
    blocks = points // block
    member = helper_flat[None, :] == jnp.arange(owners, dtype=jnp.int32)[:, None]
    member_b = member.astype(jnp.bfloat16).reshape(owners, blocks, block)
    upper = (
        jnp.arange(block, dtype=jnp.int32)[:, None] <= jnp.arange(block, dtype=jnp.int32)[None, :]
    ).astype(jnp.bfloat16)
    within = jnp.einsum("hbq,qr->hbr", member_b, upper, preferred_element_type=jnp.float32)
    totals = within[:, :, -1]
    before = (
        jnp.arange(blocks, dtype=jnp.int32)[:, None] < jnp.arange(blocks, dtype=jnp.int32)[None, :]
    ).astype(jnp.float32)
    offsets = jnp.dot(
        totals, before, precision=lax.Precision.HIGHEST, preferred_element_type=jnp.float32
    )
    inclusive = (within + offsets[:, :, None]).reshape(owners, points)
    rank = jnp.sum(jnp.where(member, inclusive - 1.0, 0.0), 0)
    return rank.astype(jnp.int32)


def per_device(
    adjoint_disp, matrix_tangent, fibre_blocks, fibre_weights, rve_class, rve_helper, rve_slot
):
    size_gx = lax.axis_size("gx")
    size_gy = lax.axis_size("gy")
    owners = size_gx * size_gy
    width_x, width_y, width_z = (
        adjoint_disp.shape[1],
        adjoint_disp.shape[2],
        adjoint_disp.shape[3],
    )
    points = width_x * width_y * width_z
    capacity = 2 * points // owners
    fibres = fibre_weights.shape[1]
    group = fibres // CLASSES
    partial_tiles = jnp.einsum(
        "ptf,ktf->tpk",
        fibre_weights.reshape(points, CLASSES, group),
        fibre_blocks.reshape(36, CLASSES, group),
        preferred_element_type=jnp.float32,
    )
    level = jnp.arange(CLASSES, dtype=jnp.int32)
    active = (rve_class[None, :] >= level[:, None]).astype(jnp.float32)
    counted = ((rve_class + 1) * group).astype(jnp.float32)
    tangent_rows = jnp.sum(partial_tiles * active[:, :, None], 0) / counted[:, None]
    corners = lift(adjoint_disp)
    grad_x = 0.25 * (corners[1].sum((0, 1)) - corners[0].sum((0, 1)))
    grad_y = 0.25 * (corners[:, 1].sum((0, 1)) - corners[:, 0].sum((0, 1)))
    grad_z = 0.25 * (corners[:, :, 1].sum((0, 1)) - corners[:, :, 0].sum((0, 1)))
    strain = jnp.stack(
        [
            grad_x[0],
            grad_y[1],
            grad_z[2],
            grad_z[1] + grad_y[2],
            grad_z[0] + grad_x[2],
            grad_y[0] + grad_x[1],
        ]
    )
    strain_flat = strain.reshape(6, points)
    helper_flat = rve_helper.reshape(points)
    slot_flat = rve_slot.reshape(points)
    position = ranks_within(helper_flat, owners, points)
    target = helper_flat * capacity + position
    source = (
        jnp.full((owners * capacity,), points, jnp.int32)
        .at[target]
        .set(jnp.arange(points, dtype=jnp.int32))
    )
    slot_padded = jnp.concatenate([slot_flat, jnp.zeros((1,), jnp.int32)])
    slot_buffer = jnp.take(slot_padded, source, axis=0).reshape(owners, 1, capacity)
    strain_padded = jnp.concatenate([strain_flat.T, jnp.zeros((1, 6), jnp.float32)], 0)
    strain_buffer = jnp.transpose(
        jnp.take(strain_padded, source, axis=0).reshape(owners, capacity, 6), (0, 2, 1)
    )
    pieces = (
        lax.all_to_all(strain_buffer, ("gx", "gy"), split_axis=0, concat_axis=0, tiled=True),
        lax.all_to_all(slot_buffer, ("gx", "gy"), split_axis=0, concat_axis=0, tiled=True),
    )
    answer = respond(tangent_rows, pieces[0], pieces[1])
    returned = lax.all_to_all(answer, ("gx", "gy"), split_axis=0, concat_axis=0, tiled=True)
    returned_rows = jnp.transpose(returned, (0, 2, 1)).reshape(owners * capacity, 6)
    fibre_part = jnp.take(returned_rows, target, axis=0).T
    matrix_part = jnp.dot(
        matrix_tangent.T,
        strain_flat,
        precision=lax.Precision.HIGHEST,
        preferred_element_type=jnp.float32,
    )
    sens = (matrix_part + fibre_part).reshape(6, width_x, width_y, width_z)
    along_x = jnp.stack([sens[0], sens[5], sens[4]])
    along_y = jnp.stack([sens[5], sens[1], sens[3]])
    along_z = jnp.stack([sens[4], sens[3], sens[2]])
    signs = jnp.array(SIGNS, jnp.float32)
    pieces = (
        signs[:, None, None, None, None, None, None] * along_x
        + signs[None, :, None, None, None, None, None] * along_y
        + signs[None, None, :, None, None, None, None] * along_z
    )
    return settle(pieces)


def solution(mesh):
    in_specs = (
        P(None, "gx", "gy", "gz"),
        P(),
        P(),
        P(("gx", "gy", "gz"), None),
        P(("gx", "gy", "gz")),
        P("gx", "gy", "gz"),
        P("gx", "gy", "gz"),
    )
    out_specs = P(None, "gx", "gy", "gz")
    return jax.shard_map(
        per_device, mesh=mesh, in_specs=in_specs, out_specs=out_specs, check_vma=False
    )
```

profile of v0, /device:TPU:46, one launch (start us, length us, event | category | flops | bytes accessed | tf_op | source)
XLA Modules:
  0.0 235.3 jit_solution(89025342010459596)
XLA Ops:
  0.0 0.0 copy-start
  0.0 0.7 slice.127
  0.7 2.0 collective-permute-start
  2.8 0.7 broadcast_multiply_fusion.3
  3.5 1.0 fusion.6
  4.5 0.3 slice.198
  4.8 0.7 copy.46
  5.5 0.2 fusion.33
  5.8 0.0 copy-done.2
  5.8 0.3 select_reduce_fusion
  6.2 15.5 %scatter_custom_fusion = s32[8192]{0:T(1024)S(1)} fusion(s32[4096]{0:T(1024)S(1)} %bitcast.118, s32[4096]{0:T(1024)S(1)} %iota.38, s32[]{:T(128)} %constant.51.clone.1), kind=kCustom, calls=%fused_computation.99 | custom fusion | bytes 32772 | tf_op jit(solution)/shard_map/scatter | solution.py:112
  21.8 0.0 copy-done.5
  21.8 0.0 copy-start.3
  21.8 0.0 copy-start.4
  21.8 45.5 %gather_fusion.1 = s32[8192]{0:T(1024)S(1)} fusion(s32[4097]{0:T(1024)S(1)} %pad_add_fusion, s32[8192]{0:T(1024)S(1)} %fusion.32), kind=kCustom, calls=%fused_computation.1 | custom fusion | bytes 98304 | tf_op jit(solution)/shard_map/jit(_take)/gather | solution.py:115
  67.4 0.6 broadcast_select_fusion
  68.0 12.1 %all-to-all-start.1 = ((s32[64,1,128]{2,1,0:T(1,128)}), s32[64,1,128]{2,1,0:T(1,128)S(1)}, u32[]{:S(2)}, u32[]{:S(2)}) async-start(s32[64,1,128]{2,1,0:T(1,128)} %bitcast.26), calls=%async_computation.1 | async-start | bytes 65536 | tf_op jit(solution)/shard_map/all_to_all | solution.py:122
  80.1 0.0 copy-done.3
  80.2 0.0 copy-start.1
  80.2 4.8 %fusion.3 = f32[4096,36]{0,1:T(8,128)S(1)} fusion(f32[4,4096]{1,0:T(4,128)S(1)} %fusion.26, bf16[36,4,128]{2,1,0:T(4,128)(2,1)S(1)} %reshape.230, bf16[4096,512]{1,0:T(8,128)(2,1)} %param.11), kind=kOutput, calls=%fused_computation.10 | convolution fusion | flops 152027136 | bytes 4886528 | tf_op jit(solution)/shard_map/ptf,ktf->tpk/dot_general | solution.py:80
  85.0 0.1 broadcast_divide_fusion
  85.0 0.6 copy.52
  85.7 0.0 collective-permute-done
  85.7 2.2 collective-permute-start.1
  88.0 1.4 collective-permute-done.1
  89.4 0.1 fusion.8
  89.5 2.7 %collective-permute-start.2 = (f32[2,2,3,4,8,1]{5,4,3,2,0,1:T(8,128)S(1)}, f32[2,2,3,4,8,1]{5,4,3,2,0,1:T(8,128)S(1)}, u32[]{:S(2)}, u32[]{:S(2)}) collective-permute-start(f32[2,2,3,4,8,1]{5,4,3,2,0,1:T(8,128)S(1)} %fusion.9), channel_id=1, source_target_pairs={{1,0},{2,1},{3,2},{5,4},{6,5},{7,6},{9,8},{10,9},{11,10},{13,12},{... | collective-permute-start | bytes 4616 | tf_op jit(solution)/shard_map/ppermute | solution.py:17
  92.3 4.7 %collective-permute-done.2 = f32[2,2,3,4,8,1]{5,4,3,2,0,1:T(8,128)S(1)} collective-permute-done((f32[2,2,3,4,8,1]{5,4,3,2,0,1:T(8,128)S(1)}, f32[2,2,3,4,8,1]{5,4,3,2,0,1:T(8,128)S(1)}, u32[]{:S(2)}, u32[]{:S(2)}) %collective-permute-start.2) | collective-permute-done | bytes 1568 | tf_op jit(solution)/shard_map/ppermute | solution.py:17
  97.0 0.1 fusion.27
  97.3 0.2 stack.69
  97.4 2.0 copy.48
  99.4 3.1 %concatenate.28 = f32[4097,6]{1,0:T(8,128)} pad(f32[4096,6]{1,0:T(8,128)} %bitcast.105, f32[]{:T(128)} %constant.38.clone.1), padding=0_1x0_0 | pad | bytes 196636 | tf_op jit(solution)/shard_map/concatenate | solution.py:116
  102.5 29.4 %gather_fusion = f32[8192,6]{1,0:T(8,128)} fusion(f32[4097,6]{1,0:T(8,128)} %concatenate.28, s32[8192]{0:T(1024)S(1)} %fusion.32), kind=kCustom, calls=%fused_computation | custom fusion | bytes 425984 | tf_op jit(solution)/shard_map/jit(_take)/gather | solution.py:118
  131.9 2.8 %copy.49 = f32[64,128,6]{1,2,0:T(8,128)S(1)} copy(f32[64,128,6]{2,1,0:T(8,128)} %bitcast.104) | data formatting | bytes 393216 | tf_op jit(solution)/shard_map/jit(_take)/gather | solution.py:118
  134.8 0.7 select_bitcast_fusion
  135.5 0.0 all-to-all-done.1
  135.5 10.5 %all-to-all-start = ((f32[64,6,128]{2,1,0:T(8,128)}), f32[64,6,128]{2,1,0:T(8,128)S(1)}, u32[]{:S(2)}, u32[]{:S(2)}) async-start(f32[64,6,128]{2,1,0:T(8,128)} %select_bitcast_fusion), calls=%async_computation | async-start | bytes 524288 | tf_op jit(solution)/shard_map/all_to_all | solution.py:121
  146.1 27.8 %gather_fusion.2 = f32[8192,36]{1,0:T(8,128)} fusion(f32[4096,36]{1,0:T(8,128)S(1)} %copy.52, s32[8192]{0:T(1024)S(1)} %broadcast_clamp_fusion), kind=kCustom, calls=%fused_computation.2 | custom fusion | bytes 2392064 | tf_op jit(solution)/shard_map/jit(_take)/gather | solution.py:40
  174.0 2.9 %copy.53 = f32[8192,36]{0,1:T(8,128)S(1)} copy(f32[8192,36]{1,0:T(8,128)} %gather_fusion.2) | data formatting | bytes 2359296 | tf_op jit(solution)/shard_map/jit(_take)/gather | solution.py:40
  176.8 0.2 copy.71
  177.1 0.1 slice.214
  177.2 0.0 all-to-all-done
  177.3 0.1 multiply_reduce_fusion
  177.5 0.8 copy.81
  178.3 10.3 %all-to-all-start.2 = ((f32[64,6,128]{2,1,0:T(8,128)}), f32[64,6,128]{2,1,0:T(8,128)S(1)}, u32[]{:S(2)}, u32[]{:S(2)}) async-start(f32[64,6,128]{2,1,0:T(8,128)} %bitcast.102), calls=%async_computation.2 | async-start | bytes 524288 | tf_op jit(solution)/shard_map/all_to_all | solution.py:125
  188.6 11.7 %all-to-all-done.2 = f32[64,6,128]{2,1,0:T(8,128)S(1)} async-done(((f32[64,6,128]{2,1,0:T(8,128)}), f32[64,6,128]{2,1,0:T(8,128)S(1)}, u32[]{:S(2)}, u32[]{:S(2)}) %all-to-all-start.2) | async-done | bytes 196640 | tf_op jit(solution)/shard_map/all_to_all | solution.py:125
  200.3 2.6 %copy.54 = f32[64,128,6]{2,1,0:T(8,128)} copy(f32[64,128,6]{1,2,0:T(8,128)S(1)} %bitcast.112) | data formatting | bytes 393216 | tf_op jit(solution)/shard_map/transpose | solution.py:126
  202.9 13.0 %gather_fusion.3 = f32[4096,6]{1,0:T(8,128)S(1)} fusion(f32[8192,6]{1,0:T(8,128)} %bitcast.103, s32[4096]{0:T(1024)S(1)} %broadcast_clamp_fusion.1), kind=kCustom, calls=%fused_computation.3 | custom fusion | bytes 212992 | tf_op jit(solution)/shard_map/jit(_take)/gather | solution.py:127
  215.9 0.0 copy-start.6
  215.9 0.6 copy.55
  216.5 0.3 fusion
  216.9 0.1 fusion.38
  217.0 0.1 broadcast_multiply_fusion.2
  217.1 0.1 slice.206
  217.3 0.3 copy.56
  217.6 1.3 collective-permute-start.3
  218.9 4.6 %collective-permute-done.3 = f32[2,2,3,4,8,1]{4,3,2,1,0,5:T(4,128)S(1)} collective-permute-done((f32[2,2,3,4,8,1]{4,3,2,1,0,5:T(4,128)S(1)}, f32[2,2,3,4,8,1]{4,3,2,1,0,5:T(4,128)S(1)}, u32[]{:S(2)}, u32[]{:S(2)}) %collective-permute-start.3) | collective-permute-done | bytes 1568 | tf_op jit(solution)/shard_map/ppermute | solution.py:17
  223.6 0.4 copy.57
  223.9 0.1 fusion.17
  224.1 1.9 collective-permute-start.4
  226.0 3.1 %collective-permute-done.4 = f32[2,3,4,1,128]{4,2,1,0,3:T(4,128)S(1)} collective-permute-done((f32[2,3,4,1,128]{4,2,1,0,3:T(4,128)S(1)}, f32[2,3,4,1,128]{4,2,1,0,3:T(4,128)S(1)}, u32[]{:S(2)}, u32[]{:S(2)}) %collective-permute-start.4) | collective-permute-done | bytes 12320 | tf_op jit(solution)/shard_map/ppermute | solution.py:17
  229.1 3.0 %collective-permute-start.5 = (f32[3,1,8,128]{3,2,0,1:T(8,128)S(1)}, f32[3,1,8,128]{3,2,0,1:T(8,128)S(1)}, u32[]{:S(2)}, u32[]{:S(2)}) collective-permute-start(f32[3,1,8,128]{3,2,0,1:T(8,128)S(1)} %slice_bitcast_fusion.6), channel_id=1, source_target_pairs={{0,32},{32,64},{64,96},{96,128},{128,160},{160,192},{192,224},{1,3... | collective-permute-start | bytes 36872 | tf_op jit(solution)/shard_map/ppermute | solution.py:17
  232.1 2.5 %collective-permute-done.5 = f32[3,1,8,128]{3,2,0,1:T(8,128)S(1)} collective-permute-done((f32[3,1,8,128]{3,2,0,1:T(8,128)S(1)}, f32[3,1,8,128]{3,2,0,1:T(8,128)S(1)}, u32[]{:S(2)}, u32[]{:S(2)}) %collective-permute-start.5) | collective-permute-done | bytes 12320 | tf_op jit(solution)/shard_map/ppermute | solution.py:17
  234.7 0.6 fusion.29
  (42 shorter events, 0.6 us)
Async XLA Ops:
  0.0 216.5 %copy-start = (f32[6,6]{1,0:T(8,128)S(1)}, f32[6,6]{1,0:T(8,128)}, u32[]{:S(2)}) copy-start(f32[6,6]{1,0:T(8,128)} %param.9) | copy-start | bytes 436
  0.0 5.8 %copy-start.2 = (s32[4,8,128]{2,1,0:T(8,128)S(1)}, s32[4,8,128]{2,1,0:T(8,128)}, u32[]{:S(2)}) copy-start(s32[4,8,128]{2,1,0:T(8,128)} %param.13) | copy-start | bytes 49156
  0.7 84.9 %collective-permute-start = (f32[3,1,8,128]{3,2,1,0:T(8,128)S(1)}, f32[3,1,8,128]{3,2,1,0:T(8,128)S(1)}, u32[]{:S(2)}, u32[]{:S(2)}) collective-permute-start(f32[3,1,8,128]{3,2,1,0:T(8,128)S(1)} %slice.127), channel_id=1, source_target_pairs={{32,0},{64,32},{96,64},{128,96},{160,128},{192,160},{224,192},{33,... | collective-permute-start | bytes 36872 | tf_op jit(solution)/shard_map/ppermute | solution.py:17
  3.5 18.3 %copy-start.5 = (s32[4,8,128]{2,1,0:T(8,128)S(1)}, s32[4,8,128]{2,1,0:T(8,128)}, u32[]{:S(2)}) copy-start(s32[4,8,128]{2,1,0:T(8,128)} %param.14) | copy-start | bytes 49156
  21.8 58.3 %copy-start.3 = (s32[4096]{0:T(1024)S(1)}, s32[4096]{0:T(1024)}, u32[]{:S(2)}) copy-start(s32[4096]{0:T(1024)} %param.12) | copy-start | bytes 49156
  21.8 58.3 %copy-start.4 = (bf16[36,512]{1,0:T(8,128)(2,1)S(1)}, bf16[36,512]{1,0:T(8,128)(2,1)}, u32[]{:S(2)}) copy-start(bf16[36,512]{1,0:T(8,128)(2,1)} %param.10) | copy-start | bytes 110596
  68.0 67.5 %all-to-all-start.1 = ((s32[64,1,128]{2,1,0:T(1,128)}), s32[64,1,128]{2,1,0:T(1,128)S(1)}, u32[]{:S(2)}, u32[]{:S(2)}) async-start(s32[64,1,128]{2,1,0:T(1,128)} %bitcast.26), calls=%async_computation.1 | async-start | bytes 65536 | tf_op jit(solution)/shard_map/all_to_all | solution.py:122
  80.2 4.8 %copy-start.1 = (f32[3,4,8,128]{3,2,1,0:T(8,128)S(1)}, f32[3,4,8,128]{3,2,1,0:T(8,128)}, u32[]{:S(2)}) copy-start(f32[3,4,8,128]{3,2,1,0:T(8,128)} %param.8) | copy-start | bytes 147460
  85.7 3.6 %collective-permute-start.1 = (f32[2,3,4,1,128]{4,3,2,1,0:T(1,128)S(1)}, f32[2,3,4,1,128]{4,3,2,1,0:T(1,128)S(1)}, u32[]{:S(2)}, u32[]{:S(2)}) collective-permute-start(f32[2,3,4,1,128]{4,3,2,1,0:T(1,128)S(1)} %fusion.37), channel_id=1, source_target_pairs={{4,0},{8,4},{12,8},{16,12},{20,16},{24,20},{28,24},{5,1},{9,5},{13... | collective-permute-start | bytes 36872 | tf_op jit(solution)/shard_map/ppermute | solution.py:17
  89.5 7.5 %collective-permute-start.2 = (f32[2,2,3,4,8,1]{5,4,3,2,0,1:T(8,128)S(1)}, f32[2,2,3,4,8,1]{5,4,3,2,0,1:T(8,128)S(1)}, u32[]{:S(2)}, u32[]{:S(2)}) collective-permute-start(f32[2,2,3,4,8,1]{5,4,3,2,0,1:T(8,128)S(1)} %fusion.9), channel_id=1, source_target_pairs={{1,0},{2,1},{3,2},{5,4},{6,5},{7,6},{9,8},{10,9},{11,10},{13,12},{... | collective-permute-start | bytes 4616 | tf_op jit(solution)/shard_map/ppermute | solution.py:17
  135.5 41.7 %all-to-all-start = ((f32[64,6,128]{2,1,0:T(8,128)}), f32[64,6,128]{2,1,0:T(8,128)S(1)}, u32[]{:S(2)}, u32[]{:S(2)}) async-start(f32[64,6,128]{2,1,0:T(8,128)} %select_bitcast_fusion), calls=%async_computation | async-start | bytes 524288 | tf_op jit(solution)/shard_map/all_to_all | solution.py:121
  178.3 22.0 %all-to-all-start.2 = ((f32[64,6,128]{2,1,0:T(8,128)}), f32[64,6,128]{2,1,0:T(8,128)S(1)}, u32[]{:S(2)}, u32[]{:S(2)}) async-start(f32[64,6,128]{2,1,0:T(8,128)} %bitcast.102), calls=%async_computation.2 | async-start | bytes 524288 | tf_op jit(solution)/shard_map/all_to_all | solution.py:125
  215.9 1.1 copy-start.6
  217.6 5.9 %collective-permute-start.3 = (f32[2,2,3,4,8,1]{4,3,2,1,0,5:T(4,128)S(1)}, f32[2,2,3,4,8,1]{4,3,2,1,0,5:T(4,128)S(1)}, u32[]{:S(2)}, u32[]{:S(2)}) collective-permute-start(f32[2,2,3,4,8,1]{4,3,2,1,0,5:T(4,128)S(1)} %bitcast.135), channel_id=1, source_target_pairs={{0,1},{1,2},{2,3},{4,5},{5,6},{6,7},{8,9},{9,10},{10,11},{12,13},{... | collective-permute-start | bytes 4616 | tf_op jit(solution)/shard_map/ppermute | solution.py:17
  224.1 5.0 %collective-permute-start.4 = (f32[2,3,4,1,128]{4,2,1,0,3:T(4,128)S(1)}, f32[2,3,4,1,128]{4,2,1,0,3:T(4,128)S(1)}, u32[]{:S(2)}, u32[]{:S(2)}) collective-permute-start(f32[2,3,4,1,128]{4,2,1,0,3:T(4,128)S(1)} %bitcast.139), channel_id=1, source_target_pairs={{0,4},{4,8},{8,12},{12,16},{16,20},{20,24},{24,28},{1,5},{5,9},{9,... | collective-permute-start | bytes 36872 | tf_op jit(solution)/shard_map/ppermute | solution.py:17
  229.1 5.6 %collective-permute-start.5 = (f32[3,1,8,128]{3,2,0,1:T(8,128)S(1)}, f32[3,1,8,128]{3,2,0,1:T(8,128)S(1)}, u32[]{:S(2)}, u32[]{:S(2)}) collective-permute-start(f32[3,1,8,128]{3,2,0,1:T(8,128)S(1)} %slice_bitcast_fusion.6), channel_id=1, source_target_pairs={{0,32},{32,64},{64,96},{96,128},{128,160},{160,192},{192,224},{1,3... | collective-permute-start | bytes 36872 | tf_op jit(solution)/shard_map/ppermute | solution.py:17
where the time goes:
time: 237 us; the launch traced here: 235 us
  local copies, waits for them, and re-layouts  150 us (63%)
  starting transfers between devices  46.1 us (19%)
  waiting for transfers between devices  28 us (12%)
  matrix products  6.34 us (3%)
  other arithmetic  4.15 us (2%)
    gather x1, local copies, waits for them, and re-layouts, per_device(): jnp.take(slot_padded, source, axis=0).reshape(owners, 1, capacity)  45.5 us
    gather x2, local copies, waits for them, and re-layouts, per_device(): jnp.take(strain_padded, source, axis=0).reshape(owners, capacity, 6)  32.3 us
    gather x2, local copies, waits for them, and re-layouts, respond(): jnp.take(tangent_rows, asked.reshape(-1), axis=0)  30.7 us
    ppermute x6, waiting for transfers between devices, passed_along(): return lax.ppermute(array, axis, pairs)  16.3 us
    scatter x1, local copies, waits for them, and re-layouts, per_device(): source = jnp.full((owners * capacity,), points, jnp.int32).at[target].set...  15.5 us
    gather x2, local copies, waits for them, and re-layouts, per_device(): fibre_part = jnp.take(returned_rows, target, axis=0).T  13.6 us
    ppermute x6, starting transfers between devices, passed_along(): return lax.ppermute(array, axis, pairs)  13.2 us
    all_to_all x1, starting transfers between devices, per_device(): lax.all_to_all(slot_buffer, ('gx', 'gy'), split_axis=0, concat_axis=0, ti...  12.1 us
  transfers between devices with their start and end apart: 9, of which 6 were waited for; matrix products, arithmetic and copies ran while one was open for 60% of the time, Pallas kernels for 0%

commit v1 on v0

v1 whole, which is shorter than its diff:
```python
import functools

import jax
import jax.numpy as jnp
from jax import lax
from jax.experimental import pallas as pl
from jax.experimental.pallas import tpu as pltpu
from jax.sharding import PartitionSpec as P

CLASSES = 4
LANES = 128
STEP = 4
SMEM = pl.BlockSpec(memory_space=pltpu.SMEM)
VMEM = pl.BlockSpec(memory_space=pltpu.VMEM)
NT = (((1,), (1,)), ((), ()))


def passed_round(array, axis, by):
    devices = lax.axis_size(axis)
    return lax.ppermute(array, axis, [(i, (i + by) % devices) for i in range(devices)])


def whole_call(kernel, name, out, inputs, scratch=(), flops=0, scalars=()):
    outs = [VMEM] * len(out) if isinstance(out, (list, tuple)) else VMEM
    return pl.pallas_call(
        kernel,
        name=name,
        out_shape=out,
        in_specs=[SMEM if i in scalars else VMEM for i in range(len(inputs))],
        out_specs=outs,
        scratch_shapes=list(scratch),
        cost_estimate=pl.CostEstimate(flops=flops, bytes_accessed=1 << 20, transcendentals=0),
        compiler_params=pltpu.CompilerParams(vmem_limit_bytes=32 << 20),
    )(*inputs)


def f32(*shape):
    return jax.ShapeDtypeStruct(shape, jnp.float32)


def i32(*shape):
    return jax.ShapeDtypeStruct(shape, jnp.int32)


def iota(shape, dim):
    return lax.broadcasted_iota(jnp.int32, shape, dim)


def halves(table):
    high = table.astype(jnp.bfloat16)
    low = (table - high.astype(jnp.float32)).astype(jnp.bfloat16)
    return jnp.concatenate([high, low], 1)


def one_hot(low):
    return jnp.where(iota((LANES, LANES), 0) == low, 1.0, 0.0).astype(jnp.bfloat16)


def looked_up(table, highs, columns, start):
    products = jnp.dot(
        table, jnp.concatenate([columns, columns], 0), preferred_element_type=jnp.float32
    )
    found = []
    for i, high in enumerate(highs):
        total = jnp.full((8, LANES), start, jnp.float32)
        for row in range(table.shape[0] // 8):
            part = products[8 * row : 8 * row + 8, LANES * i : LANES * (i + 1)]
            total = jnp.where(high == row, part, total)
        found.append(total)
    return found


def spread(row):
    return jnp.broadcast_to(row, (8, LANES))


def transposed_lanes(block):
    gap = LANES - block.shape[0]
    if gap:
        block = jnp.concatenate([block, jnp.zeros((gap, LANES), block.dtype)], 0)
    return block.T


def first_layer_kernel(disp_ref, out_ref):
    out_ref[...] = transposed_lanes(disp_ref[...])[0:8]


def route_kernel(owners, helper_ref, source_ref, target_ref, member_ref, ranks_ref):
    blocks = helper_ref.shape[0]
    upper = (iota((LANES, 2 * LANES), 0) <= iota((LANES, 2 * LANES), 1)).astype(jnp.bfloat16)
    owner = iota((owners, LANES), 0)
    lane = iota((owners, LANES), 1)
    place = iota((LANES, LANES), 0)
    before = jnp.zeros((owners, LANES), jnp.float32)
    for block in range(blocks):
        helper = helper_ref[pl.ds(block, 1), :]
        member = helper == owner
        counted = jnp.dot(
            jnp.where(member, 1.0, 0.0).astype(jnp.bfloat16),
            upper,
            preferred_element_type=jnp.float32,
        )
        rank = before + counted[:, :LANES] - 1.0
        rank = jnp.sum(jnp.where(member, rank, 0.0), 0, keepdims=True).astype(jnp.int32)
        before = before + counted[:, LANES:]
        target_ref[pl.ds(block, 1), :] = helper * LANES + rank
        columns = pl.ds(block * LANES, LANES)
        member_ref[pl.ds(0, owners), columns] = jnp.where(member, float(block), 0.0).astype(
            jnp.bfloat16
        )
        member_ref[pl.ds(owners, owners), columns] = jnp.where(
            member, (lane + 1).astype(jnp.float32), 0.0
        ).astype(jnp.bfloat16)
        ranks_ref[:, columns] = jnp.where(place == rank, 1.0, 0.0).astype(jnp.bfloat16)
    found = lax.dot_general(
        member_ref[...], ranks_ref[...], NT, preferred_element_type=jnp.float32
    ).astype(jnp.int32)
    source_ref[...] = found[:owners] * LANES + found[owners:] - 1


def strain_kernel(
    owners,
    width_x,
    inside_ref,
    disp_ref,
    first_ref,
    side_ref,
    next_ref,
    source_ref,
    slot_ref,
    out_ref,
    field_ref,
):
    planes = width_x
    in_x, in_y, in_z = (inside_ref[i] != 0 for i in range(3))
    edges = transposed_lanes(
        jnp.concatenate(
            [
                first_ref[0:1],
                side_ref[24:25],
                next_ref[15:16],
                next_ref[16:17],
                jnp.zeros((4, LANES), jnp.float32),
            ],
            0,
        )
    )
    sums = {}
    for c in range(3):
        for x in range(planes + 1):
            k = c * planes + x
            if x < planes:
                here = disp_ref[pl.ds(8 * k, 8), :]
                above = next_ref[pl.ds(k, 1), :]
                spot, column = 8 * k, 0
            else:
                here = side_ref[pl.ds(8 * c, 8), :]
                above = next_ref[pl.ds(3 * planes + c, 1), :]
                spot, column = 8 * c * planes, 1
            edge = jnp.where(in_z, edges[spot : spot + 8, column : column + 1], 0.0)
            corner = jnp.where(in_z, edges[spot : spot + 1, column + 2 : column + 3], 0.0)
            if x == planes:
                here, edge = jnp.where(in_x, here, 0.0), jnp.where(in_x, edge, 0.0)
                above, corner = jnp.where(in_x, above, 0.0), jnp.where(in_x, corner, 0.0)
            above, corner = jnp.where(in_y, above, 0.0), jnp.where(in_y, corner, 0.0)
            here_z = jnp.concatenate([here[:, 1:], edge], 1)
            there = jnp.concatenate([here[1:], above], 0)
            there_z = jnp.concatenate([here_z[1:], jnp.concatenate([above[:, 1:], corner], 1)], 0)
            low, high = here + here_z, there + there_z
            sums[c, x] = (low + high, high - low, (here_z - here) + (there_z - there))
    for x in range(planes):
        grad_x = [0.25 * (sums[c, x + 1][0] - sums[c, x][0]) for c in range(3)]
        grad_y = [0.25 * (sums[c, x + 1][1] + sums[c, x][1]) for c in range(3)]
        grad_z = [0.25 * (sums[c, x + 1][2] + sums[c, x][2]) for c in range(3)]
        slot = slot_ref[pl.ds(8 * x, 8), :].astype(jnp.float32)
        fields = (
            grad_x[0],
            grad_y[1],
            grad_z[2],
            grad_z[1] + grad_y[2],
            grad_z[0] + grad_x[2],
            grad_y[0] + grad_x[1],
            slot,
            slot,
        )
        for f, field in enumerate(fields):
            field_ref[pl.ds(64 * x + f, 8, stride=8), :] = field
    table = halves(field_ref[...])
    for owner in range(0, owners, STEP):
        rows = [source_ref[pl.ds(o, 1), :] for o in range(owner, owner + STEP)]
        columns = jnp.concatenate([one_hot(row & (LANES - 1)) for row in rows], 1)
        found = looked_up(table, [spread(row >> 7) for row in rows], columns, -1.0)
        for i in range(STEP):
            out_ref[owner + i] = found[i]


def tangent_kernel(weights_ref, class_ref, blocks_ref, matrix_ref, out_ref):
    points = weights_ref.shape[0]
    fibres = blocks_ref[...].astype(jnp.float32)
    gap = jnp.zeros((2, fibres.shape[1]), jnp.float32)
    pieces = []
    for m in range(6):
        pieces += [fibres[6 * m : 6 * m + 6], gap]
    fibres = jnp.concatenate(pieces, 0).astype(jnp.bfloat16)
    row = iota((8, LANES), 0)
    matrix = []
    for m in range(6):
        column = jnp.zeros((8, LANES), jnp.float32)
        for n in range(6):
            column = jnp.where(row == n, matrix_ref[m, n], column)
        matrix.append(column)
    matrix = jnp.concatenate(matrix, 0)
    chunk = 1024
    for start in range(0, points, chunk):
        parts = []
        for group in range(CLASSES):
            columns = slice(LANES * group, LANES * (group + 1))
            parts.append(
                lax.dot_general(
                    fibres[:, columns],
                    weights_ref[pl.ds(start, chunk), columns],
                    NT,
                    preferred_element_type=jnp.float32,
                )
            )
        for block in range(chunk // LANES):
            lanes = slice(LANES * block, LANES * (block + 1))
            level = class_ref[pl.ds(start // LANES + block, 1), :]
            total = parts[0][:, lanes]
            for group in range(1, CLASSES):
                total = total + jnp.where(level >= group, parts[group][:, lanes], 0.0)
            scale = 1.0 / ((level + 1) * LANES).astype(jnp.float32)
            out_ref[:, pl.ds(start + LANES * block, LANES)] = total * scale + matrix


def respond_kernel(arrived_ref, tangent_ref, out_ref, member_ref, lows_ref, answer_ref):
    owners = arrived_ref.shape[0]
    blocks = tangent_ref.shape[1] // LANES
    rows = iota((blocks, LANES), 0)
    lane = (iota((blocks, LANES), 1) + 1).astype(jnp.float32)
    slots = []
    for sender in range(owners):
        slot = arrived_ref[sender, 6:7, :].astype(jnp.int32)
        slots.append(slot)
        named = rows == (slot >> 7)
        columns = pl.ds(sender * LANES, LANES)
        member_ref[pl.ds(0, blocks), columns] = jnp.where(named, float(sender), 0.0).astype(
            jnp.bfloat16
        )
        member_ref[pl.ds(blocks, blocks), columns] = jnp.where(named, lane, 0.0).astype(jnp.bfloat16)
        lows_ref[:, columns] = one_hot(slot & (LANES - 1))
    where = lax.dot_general(
        member_ref[...], lows_ref[...], NT, preferred_element_type=jnp.float32
    ).astype(jnp.int32)

    table = halves(arrived_ref[...].reshape(8 * owners, LANES))
    for block in range(0, blocks, STEP):
        steps = range(block, block + STEP)
        columns = jnp.concatenate([one_hot(where[blocks + b : blocks + b + 1] - 1) for b in steps], 1)
        found = looked_up(table, [spread(where[b : b + 1]) for b in steps], columns, 0.0)
        for i, b in enumerate(steps):
            total = jnp.zeros((8, LANES), jnp.float32)
            for m in range(6):
                tangent = tangent_ref[pl.ds(8 * m, 8), pl.ds(b * LANES, LANES)]
                total = total + tangent * spread(found[i][m : m + 1])
            answer_ref[pl.ds(8 * b, 8), :] = total

    table = halves(answer_ref[...])
    for sender in range(0, owners, STEP):
        columns = lows_ref[:, pl.ds(sender * LANES, STEP * LANES)]
        highs = [spread(slot >> 7) for slot in slots[sender : sender + STEP]]
        found = looked_up(table, highs, columns, 0.0)
        for i in range(STEP):
            out_ref[sender + i] = found[i]


def collect_kernel(returned_ref, target_ref, sens_ref, last_ref, point_ref):
    owners = returned_ref.shape[0]
    blocks = target_ref.shape[0]
    table = halves(returned_ref[...].reshape(8 * owners, LANES))
    for block in range(0, blocks, STEP):
        rows = [target_ref[pl.ds(b, 1), :] for b in range(block, block + STEP)]
        columns = jnp.concatenate([one_hot(row & (LANES - 1)) for row in rows], 1)
        found = looked_up(table, [spread(row >> 7) for row in rows], columns, 0.0)
        for i in range(STEP):
            point_ref[pl.ds(8 * (block + i), 8), :] = found[i]
    for f in range(6):
        sens_ref[pl.ds(blocks * f, blocks), :] = point_ref[pl.ds(f, blocks, stride=8), :]
    half = 3 * blocks
    for part in range(2):
        turned = transposed_lanes(sens_ref[pl.ds(half * part, half), :])
        last_ref[pl.ds(part, 1), :] = turned[LANES - 1 : LANES]
    last_ref[pl.ds(2, 6), :] = jnp.zeros((6, LANES), jnp.float32)


def force_kernel(width_x, inside_ref, sens_ref, last_ref, side_ref, prior_ref, out_ref):
    planes = width_x
    blocks = 8 * planes
    fields = 6
    in_x, in_y, in_z = (inside_ref[i] != 0 for i in range(3, 6))
    rows = jnp.concatenate(
        [
            last_ref[0:2],
            side_ref[48:50],
            prior_ref[30:34],
        ],
        0,
    )
    edges = transposed_lanes(rows)
    sums = {}
    for f in range(fields):
        for x in range(-1, planes):
            part, g = f // 3, f % 3
            if x >= 0:
                here = sens_ref[pl.ds(blocks * f + 8 * x, 8), :]
                above = prior_ref[pl.ds(planes * f + x, 1), :]
                spot, column = blocks * g + 8 * x, part
            else:
                here = side_ref[pl.ds(8 * f, 8), :]
                above = prior_ref[pl.ds(planes * fields + f, 1), :]
                spot, column = blocks * g + 8 * (planes - 1), part + 2
            edge = jnp.where(in_z, edges[spot : spot + 8, column : column + 1], 0.0)
            corner = jnp.where(in_z, edges[spot + 7 : spot + 8, column + 4 : column + 5], 0.0)
            if x < 0:
                here, edge = jnp.where(in_x, here, 0.0), jnp.where(in_x, edge, 0.0)
                above, corner = jnp.where(in_x, above, 0.0), jnp.where(in_x, corner, 0.0)
            above, corner = jnp.where(in_y, above, 0.0), jnp.where(in_y, corner, 0.0)
            here_z = jnp.concatenate([edge, here[:, :-1]], 1)
            there = jnp.concatenate([above, here[:-1]], 0)
            there_z = jnp.concatenate([jnp.concatenate([corner, above[:, :-1]], 1), here_z[:-1]], 0)
            low, high = there + there_z, here + here_z
            sums[f, x] = (low + high, low - high, (here_z - here) + (there_z - there))

    def both(f, x, kind):
        return sums[f, x][kind] + sums[f, x - 1][kind]

    def jump(f, x):
        return sums[f, x - 1][0] - sums[f, x][0]

    along = ((0, 5, 4), (5, 1, 3), (4, 3, 2))
    for d in range(3):
        for x in range(planes):
            force = jump(along[d][0], x) + both(along[d][1], x, 1) + both(along[d][2], x, 2)
            out_ref[pl.ds(blocks * d + 8 * x, 8), :] = 0.25 * force


def per_device(
    adjoint_disp, matrix_tangent, fibre_blocks, fibre_weights, rve_class, rve_helper, rve_slot
):
    owners = lax.axis_size("gx") * lax.axis_size("gy")
    width_x, width_y, width_z = adjoint_disp.shape[1:]
    points = width_x * width_y * width_z
    blocks = points // LANES
    fibres = fibre_weights.shape[1]
    disp = adjoint_disp.reshape(3 * blocks, LANES)
    helper = rve_helper.reshape(blocks, LANES)
    slot = rve_slot.reshape(blocks, LANES)

    places = [lax.axis_index(axis) for axis in ("gx", "gy", "gz")]
    ends = [lax.axis_size(axis) - 1 for axis in ("gx", "gy", "gz")]
    inside = jnp.stack(
        [place < end for place, end in zip(places, ends)] + [place > 0 for place in places]
    ).astype(jnp.int32)

    with jax.named_scope("lift"):
        first = whole_call(first_layer_kernel, "first_layer", f32(8, LANES), (disp,))
        first = passed_round(first, "gz", -1)
        side = jnp.concatenate([adjoint_disp[:, 0].reshape(24, LANES), first], 0)
        side = passed_round(side, "gx", -1)
        next_y = jnp.concatenate(
            [
                adjoint_disp[:, :, 0].reshape(3 * width_x, LANES),
                side[0:24:8],
                first[0:1],
                side[24:25],
            ],
            0,
        )
        next_y = passed_round(next_y, "gy", -1)

    with jax.named_scope("route"):
        source, target = whole_call(
            functools.partial(route_kernel, owners),
            "route",
            [i32(owners, LANES), i32(blocks, LANES)],
            (helper,),
            [
                pltpu.VMEM((2 * owners, points), jnp.bfloat16),
                pltpu.VMEM((LANES, points), jnp.bfloat16),
            ],
            flops=2 * points * LANES * 2 * owners,
        )

    with jax.named_scope("strain"):
        buckets = whole_call(
            functools.partial(strain_kernel, owners, width_x),
            "strain",
            f32(owners, 8, LANES),
            (inside, disp, first, side, next_y, source, slot),
            [pltpu.VMEM((8 * blocks, LANES), jnp.float32)],
            scalars=(0,),
        )

    with jax.named_scope("tangent"):
        tangent = whole_call(
            tangent_kernel,
            "tangent",
            f32(48, points),
            (fibre_weights, rve_class.reshape(blocks, LANES), fibre_blocks, matrix_tangent),
            flops=2 * 256 * points * fibres,
            scalars=(3,),
        )

    with jax.named_scope("exchange"):
        arrived = lax.all_to_all(buckets, ("gx", "gy"), split_axis=0, concat_axis=0, tiled=True)

    with jax.named_scope("respond"):
        answer = whole_call(
            respond_kernel,
            "respond",
            f32(owners, 8, LANES),
            (arrived, tangent),
            [
                pltpu.VMEM((2 * blocks, owners * LANES), jnp.bfloat16),
                pltpu.VMEM((LANES, owners * LANES), jnp.bfloat16),
                pltpu.VMEM((8 * blocks, LANES), jnp.float32),
            ],
        )

    with jax.named_scope("return"):
        returned = lax.all_to_all(answer, ("gx", "gy"), split_axis=0, concat_axis=0, tiled=True)

    with jax.named_scope("collect"):
        sens, last = whole_call(
            collect_kernel,
            "collect",
            [f32(6 * blocks, LANES), f32(8, LANES)],
            (returned, target),
            [pltpu.VMEM((8 * blocks, LANES), jnp.float32)],
        )

    with jax.named_scope("settle"):
        sens_grid = sens.reshape(6, width_x, width_y, LANES)
        last = passed_round(last, "gz", 1)
        side = jnp.concatenate([sens_grid[:, -1].reshape(48, LANES), last], 0)
        side = passed_round(side, "gx", 1)
        prior = jnp.concatenate(
            [
                sens_grid[:, :, -1].reshape(6 * width_x, LANES),
                side[7:48:8],
                last[0:2],
                side[48:50],
            ],
            0,
        )
        prior = passed_round(prior, "gy", 1)
        force = whole_call(
            functools.partial(force_kernel, width_x),
            "force",
            f32(3 * blocks, LANES),
            (inside, sens, last, side, prior),
            scalars=(0,),
        )
    return force.reshape(3, width_x, width_y, width_z)


def solution(mesh):
    in_specs = (
        P(None, "gx", "gy", "gz"),
        P(),
        P(),
        P(("gx", "gy", "gz"), None),
        P(("gx", "gy", "gz")),
        P("gx", "gy", "gz"),
        P("gx", "gy", "gz"),
    )
    out_specs = P(None, "gx", "gy", "gz")
    return jax.shard_map(
        per_device, mesh=mesh, in_specs=in_specs, out_specs=out_specs, check_vma=False
    )
```

time: 237 us -> 80.3 us (0.34)
  the two profiles are of different devices: /device:TPU:46 before, /device:TPU:6 now
where the time goes in v1:
time: 80.3 us; the launch traced here: 79.8 us
  waiting for transfers between devices  24 us (30%)
  blocking collectives  17.7 us (22%)
  starting transfers between devices  16.6 us (21%)
  Pallas kernels  13.8 us (17%)
  local copies, waits for them, and re-layouts  7.59 us (9%)
    all_to_all x1, blocking collectives, per_device(): lax.all_to_all(answer, ('gx', 'gy'), split_axis=0, concat_axis=0, tiled=T...  17.7 us
    ppermute x6, waiting for transfers between devices, passed_round(): lax.ppermute(array, axis, [(i, (i + by) % devices) for i in range(devices)])  17.5 us
    pallas_call x7, Pallas kernels, whole_call(): pl.pallas_call(kernel, name=name, out_shape=out, in_specs=[SMEM if i in s...  13.8 us
    all_to_all x1, starting transfers between devices, per_device(): lax.all_to_all(buckets, ('gx', 'gy'), split_axis=0, concat_axis=0, tiled=...  8.58 us
    ppermute x6, starting transfers between devices, passed_round(): lax.ppermute(array, axis, [(i, (i + by) % devices) for i in range(devices)])  8.05 us
    unnamed x16, local copies, waits for them, and re-layouts  7.39 us
    all_to_all x1, waiting for transfers between devices, per_device(): lax.all_to_all(buckets, ('gx', 'gy'), split_axis=0, concat_axis=0, tiled=...  6.42 us
  transfers between devices with their start and end apart: 7, of which 6 were waited for; matrix products, arithmetic and copies ran while one was open for 0% of the time, Pallas kernels for 4%

profile of v1, /device:TPU:6, one launch (start us, length us, event | category | flops | bytes accessed | tf_op | source)
XLA Modules:
  0.0 79.8 jit_solution(11278272798344375525)
XLA Ops:
  0.0 0.0 copy-start.1
  0.0 0.8 copy-done.1
  0.8 0.1 first_layer.1
  0.9 0.9 %collective-permute-start = (f32[8,128]{1,0:T(8,128)S(1)}, f32[8,128]{1,0:T(8,128)S(1)}, u32[]{:S(2)}, u32[]{:S(2)}) collective-permute-start(f32[8,128]{1,0:T(8,128)S(1)} %first_layer.1), channel_id=1, source_target_pairs={{0,3},{1,0},{2,1},{3,2},{4,7},{5,4},{6,5},{7,6},{8,11},{9,8},{10,9... | collective-permute-start | bytes 12296 | tf_op jit(solution)/shard_map/lift/ppermute | solution.py:20
  1.7 4.0 %collective-permute-done.first_ref = f32[8,128]{1,0:T(8,128)S(1)} collective-permute-done((f32[8,128]{1,0:T(8,128)S(1)}, f32[8,128]{1,0:T(8,128)S(1)}, u32[]{:S(2)}, u32[]{:S(2)}) %collective-permute-start) | collective-permute-done | bytes 4128 | tf_op jit(solution)/shard_map/lift/ppermute | solution.py:20
  5.7 5.9 %collective-permute-start.1 = (f32[32,128]{1,0:T(8,128)S(1)}, f32[32,128]{1,0:T(8,128)S(1)}, u32[]{:S(2)}, u32[]{:S(2)}) collective-permute-start(f32[32,128]{1,0:T(8,128)S(1)} %pad_maximum_fusion.2), channel_id=1, source_target_pairs={{0,224},{32,0},{64,32},{96,64},{128,96},{160,128},{192,160},{224,1... | collective-permute-start | bytes 49160 | tf_op jit(solution)/shard_map/lift/ppermute | solution.py:20
  11.6 0.1 stack.27
  11.7 1.3 %collective-permute-done.1.side_ref = f32[32,128]{1,0:T(8,128)S(1)} collective-permute-done((f32[32,128]{1,0:T(8,128)S(1)}, f32[32,128]{1,0:T(8,128)S(1)}, u32[]{:S(2)}, u32[]{:S(2)}) %collective-permute-start.1) | collective-permute-done | bytes 16416 | tf_op jit(solution)/shard_map/lift/ppermute | solution.py:20
  13.0 0.5 collective-permute-start.2
  13.5 0.0 copy-start.7
  13.5 0.7 copy-done.7
  14.2 1.2 %route.1 = (s32[64,128]{1,0:T(8,128)S(1)}, s32[32,128]{1,0:T(8,128)S(1)}) custom-call(s32[32,128]{1,0:T(8,128)S(1)} %bitcast.28), custom_call_target="tpu_custom_call" | custom-call | flops 134217728 | bytes 1048576 | tf_op jit(solution)/shard_map/route/route/pallas_call | solution.py:25
  15.4 0.0 collective-permute-done.2.next_ref
  15.4 0.0 copy-start.2
  15.4 0.8 copy-done.2
  16.2 0.0 copy-start.5
  16.2 0.7 copy-done.5
  16.9 3.1 %strain.1 = f32[64,8,128]{2,1,0:T(8,128)} custom-call(s32[6]{0:T(128)S(1)} %convert_element_type.3.inside_ref, f32[96,128]{1,0:T(8,128)S(1)} %bitcast.23, f32[8,128]{1,0:T(8,128)S(1)} %collective-permute-done.first_ref, f32[32,128]{1,0:T(8,128)S(1)} %collective-permute-done.1.side_ref, f32[17,128]{1,0:T(8,128)S(1)} %collective-permute-done.2.next_ref, ...), custom_call_target="tpu_custom_call" | custom-call | bytes 1048576 | tf_op jit(solution)/shard_map/strain/strain/pallas_call | solution.py:25
  20.0 8.6 %all-to-all-start = ((f32[64,8,128]{2,1,0:T(8,128)}), f32[64,8,128]{2,1,0:T(8,128)S(1)}, u32[]{:S(2)}, u32[]{:S(2)}) async-start(f32[64,8,128]{2,1,0:T(8,128)} %strain.1), calls=%async_computation | async-start | bytes 524288 | tf_op jit(solution)/shard_map/exchange/all_to_all | solution.py:415
  28.6 0.0 copy-start
  28.6 2.2 %copy-done = bf16[4096,512]{1,0:T(8,128)(2,1)S(1)} copy-done((bf16[4096,512]{1,0:T(8,128)(2,1)S(1)}, bf16[4096,512]{1,0:T(8,128)(2,1)}, u32[]{:S(2)}) %copy-start) | copy-done | bytes 4194328
  30.8 0.0 copy-start.3
  30.8 0.8 copy-done.3
  31.6 0.0 copy-start.4
  31.6 0.7 copy-done.4
  32.3 0.0 copy-start.6
  32.3 0.7 copy-done.6
  33.0 2.2 %tangent.1.tangent_ref = f32[48,4096]{1,0:T(8,128)S(1)} custom-call(bf16[4096,512]{1,0:T(8,128)(2,1)S(1)} %copy-done, s32[32,128]{1,0:T(8,128)S(1)} %bitcast.26, bf16[36,512]{1,0:T(8,128)(2,1)S(1)} %copy-done.3, f32[6,6]{1,0:T(8,128)S(1)} %copy-done.6), custom_call_target="tpu_custom_call" | custom-call | flops 1073741824 | bytes 1048576 | tf_op jit(solution)/shard_map/tangent/tangent/pallas_call | solution.py:25
  35.1 6.4 %all-to-all-done.arrived_ref = f32[64,8,128]{2,1,0:T(8,128)S(1)} async-done(((f32[64,8,128]{2,1,0:T(8,128)}), f32[64,8,128]{2,1,0:T(8,128)S(1)}, u32[]{:S(2)}, u32[]{:S(2)}) %all-to-all-start) | async-done | bytes 262176 | tf_op jit(solution)/shard_map/exchange/all_to_all | solution.py:415
  41.6 4.4 %respond.1 = f32[64,8,128]{2,1,0:T(8,128)S(1)} custom-call(f32[64,8,128]{2,1,0:T(8,128)S(1)} %all-to-all-done.arrived_ref, f32[48,4096]{1,0:T(8,128)S(1)} %tangent.1.tangent_ref), custom_call_target="tpu_custom_call" | custom-call | bytes 1048576 | tf_op jit(solution)/shard_map/respond/respond/pallas_call | solution.py:25
  45.9 17.7 %all_to_all.10.returned_ref = f32[64,8,128]{2,1,0:T(8,128)S(1)} all-to-all(f32[64,8,128]{2,1,0:T(8,128)S(1)} %respond.1), channel_id=1, replica_groups=mesh['gx'=8,'gy'=8,'gz'=4] {'gx','gy'}, dimensions={0} | all-to-all | bytes 524288 | tf_op jit(solution)/shard_map/return/all_to_all | solution.py:431
  63.6 1.5 %collect.1 = (f32[192,128]{1,0:T(8,128)S(1)}, f32[8,128]{1,0:T(8,128)S(1)}) custom-call(f32[64,8,128]{2,1,0:T(8,128)S(1)} %all_to_all.10.returned_ref, s32[32,128]{1,0:T(8,128)S(1)} %get-tuple-element.10.target_ref), custom_call_target="tpu_custom_call" | custom-call | bytes 1048576 | tf_op jit(solution)/shard_map/collect/collect/pallas_call | solution.py:25
  65.1 0.1 collective-permute-start.3
  65.2 3.6 %collective-permute-done.3.last_ref = f32[8,128]{1,0:T(8,128)S(1)} collective-permute-done((f32[8,128]{1,0:T(8,128)S(1)}, f32[8,128]{1,0:T(8,128)S(1)}, u32[]{:S(2)}, u32[]{:S(2)}) %collective-permute-start.3) | collective-permute-done | bytes 4128 | tf_op jit(solution)/shard_map/settle/ppermute | solution.py:20
  68.8 0.8 collective-permute-start.4
  69.6 4.3 %collective-permute-done.4.side_ref = f32[56,128]{1,0:T(8,128)S(1)} collective-permute-done((f32[56,128]{1,0:T(8,128)S(1)}, f32[56,128]{1,0:T(8,128)S(1)}, u32[]{:S(2)}, u32[]{:S(2)}) %collective-permute-start.4) | collective-permute-done | bytes 28704 | tf_op jit(solution)/shard_map/settle/ppermute | solution.py:20
  73.9 0.0 collective-permute-start.5
  73.9 4.4 %collective-permute-done.5.prior_ref = f32[34,128]{1,0:T(8,128)S(1)} collective-permute-done((f32[34,128]{1,0:T(8,128)S(1)}, f32[34,128]{1,0:T(8,128)S(1)}, u32[]{:S(2)}, u32[]{:S(2)}) %collective-permute-start.5) | collective-permute-done | bytes 17440 | tf_op jit(solution)/shard_map/settle/ppermute | solution.py:20
  78.4 1.4 %force.1 = f32[96,128]{1,0:T(8,128)} custom-call(s32[6]{0:T(128)S(1)} %convert_element_type.3.inside_ref, f32[192,128]{1,0:T(8,128)S(1)} %get-tuple-element.11.sens_ref, f32[8,128]{1,0:T(8,128)S(1)} %collective-permute-done.3.last_ref, f32[56,128]{1,0:T(8,128)S(1)} %collective-permute-done.4.side_ref, f32[34,128]{1,0:T(8,128)S(1)} %collective-permute-done.5.prior_ref), custom_call_target="tpu_custom_call" | custom-call | bytes 1048576 | tf_op jit(solution)/shard_map/settle/force/pallas_call | solution.py:25
  (16 shorter events, 0.1 us)
Async XLA Ops:
  0.0 0.8 %copy-start.1 = (f32[3,4,8,128]{3,2,1,0:T(8,128)S(1)}, f32[3,4,8,128]{3,2,1,0:T(8,128)}, u32[]{:S(2)}) copy-start(f32[3,4,8,128]{3,2,1,0:T(8,128)} %param.7) | copy-start | bytes 147460
  0.9 4.9 %collective-permute-start = (f32[8,128]{1,0:T(8,128)S(1)}, f32[8,128]{1,0:T(8,128)S(1)}, u32[]{:S(2)}, u32[]{:S(2)}) collective-permute-start(f32[8,128]{1,0:T(8,128)S(1)} %first_layer.1), channel_id=1, source_target_pairs={{0,3},{1,0},{2,1},{3,2},{4,7},{5,4},{6,5},{7,6},{8,11},{9,8},{10,9... | collective-permute-start | bytes 12296 | tf_op jit(solution)/shard_map/lift/ppermute | solution.py:20
  5.7 7.3 %collective-permute-start.1 = (f32[32,128]{1,0:T(8,128)S(1)}, f32[32,128]{1,0:T(8,128)S(1)}, u32[]{:S(2)}, u32[]{:S(2)}) collective-permute-start(f32[32,128]{1,0:T(8,128)S(1)} %pad_maximum_fusion.2), channel_id=1, source_target_pairs={{0,224},{32,0},{64,32},{96,64},{128,96},{160,128},{192,160},{224,1... | collective-permute-start | bytes 49160 | tf_op jit(solution)/shard_map/lift/ppermute | solution.py:20
  13.0 2.4 %collective-permute-start.2 = (f32[17,128]{1,0:T(8,128)S(1)}, f32[17,128]{1,0:T(8,128)S(1)}, u32[]{:S(2)}, u32[]{:S(2)}) collective-permute-start(f32[17,128]{1,0:T(8,128)S(1)} %pad_maximum_fusion.3), channel_id=1, source_target_pairs={{0,28},{4,0},{8,4},{12,8},{16,12},{20,16},{24,20},{28,24},{1,29},{... | collective-permute-start | bytes 26120 | tf_op jit(solution)/shard_map/lift/ppermute | solution.py:20
  13.5 0.7 copy-start.7
  15.4 0.8 %copy-start.2 = (f32[3,4,8,128]{3,2,1,0:T(8,128)S(1)}, f32[3,4,8,128]{3,2,1,0:T(8,128)}, u32[]{:S(2)}) copy-start(f32[3,4,8,128]{3,2,1,0:T(8,128)} %param.7) | copy-start | bytes 147460
  16.2 0.7 copy-start.5
  20.0 21.5 %all-to-all-start = ((f32[64,8,128]{2,1,0:T(8,128)}), f32[64,8,128]{2,1,0:T(8,128)S(1)}, u32[]{:S(2)}, u32[]{:S(2)}) async-start(f32[64,8,128]{2,1,0:T(8,128)} %strain.1), calls=%async_computation | async-start | bytes 524288 | tf_op jit(solution)/shard_map/exchange/all_to_all | solution.py:415
  28.6 2.2 %copy-start = (bf16[4096,512]{1,0:T(8,128)(2,1)S(1)}, bf16[4096,512]{1,0:T(8,128)(2,1)}, u32[]{:S(2)}) copy-start(bf16[4096,512]{1,0:T(8,128)(2,1)} %weights_ref.1) | copy-start | bytes 12582916
  30.8 0.8 copy-start.3
  31.6 0.7 copy-start.4
  32.3 0.7 copy-start.6
  65.1 3.7 %collective-permute-start.3 = (f32[8,128]{1,0:T(8,128)S(1)}, f32[8,128]{1,0:T(8,128)S(1)}, u32[]{:S(2)}, u32[]{:S(2)}) collective-permute-start(f32[8,128]{1,0:T(8,128)S(1)} %get-tuple-element.12), channel_id=1, source_target_pairs={{0,1},{1,2},{2,3},{3,0},{4,5},{5,6},{6,7},{7,4},{8,9},{9,10},{10,1... | collective-permute-start | bytes 12296 | tf_op jit(solution)/shard_map/settle/ppermute | solution.py:20
  68.8 5.1 %collective-permute-start.4 = (f32[56,128]{1,0:T(8,128)S(1)}, f32[56,128]{1,0:T(8,128)S(1)}, u32[]{:S(2)}, u32[]{:S(2)}) collective-permute-start(f32[56,128]{1,0:T(8,128)S(1)} %pad_maximum_fusion), channel_id=1, source_target_pairs={{0,32},{32,64},{64,96},{96,128},{128,160},{160,192},{192,224},{224... | collective-permute-start | bytes 86024 | tf_op jit(solution)/shard_map/settle/ppermute | solution.py:20
  73.9 4.4 %collective-permute-start.5 = (f32[34,128]{1,0:T(8,128)S(1)}, f32[34,128]{1,0:T(8,128)S(1)}, u32[]{:S(2)}, u32[]{:S(2)}) collective-permute-start(f32[34,128]{1,0:T(8,128)S(1)} %pad_maximum_fusion.1), channel_id=1, source_target_pairs={{0,4},{4,8},{8,12},{12,16},{16,20},{20,24},{24,28},{28,0},{1,5},{5... | collective-permute-start | bytes 52232 | tf_op jit(solution)/shard_map/settle/ppermute | solution.py:20

commit v2 on v1

--- a/solution.py
+++ b/solution.py
@@ -11,6 +11,7 @@
 LANES = 128
 STEP = 4
 SMEM = pl.BlockSpec(memory_space=pltpu.SMEM)
+HBM = pl.BlockSpec(memory_space=pltpu.HBM)
 VMEM = pl.BlockSpec(memory_space=pltpu.VMEM)
 NT = (((1,), (1,)), ((), ()))
 
@@ -20,17 +21,22 @@
     return lax.ppermute(array, axis, [(i, (i + by) % devices) for i in range(devices)])
 
 
-def whole_call(kernel, name, out, inputs, scratch=(), flops=0, scalars=()):
-    outs = [VMEM] * len(out) if isinstance(out, (list, tuple)) else VMEM
+def exchanged(array, owners, axes):
+    flat = array.reshape(owners, 1, -1)
+    flat = lax.all_to_all(flat, axes, split_axis=0, concat_axis=0, tiled=True)
+    return flat.reshape(array.shape)
+
+
+def whole_call(kernel, name, out, inputs, scratch=(), flops=0, places=None):
     return pl.pallas_call(
         kernel,
         name=name,
         out_shape=out,
-        in_specs=[SMEM if i in scalars else VMEM for i in range(len(inputs))],
-        out_specs=outs,
+        in_specs=places or [VMEM] * len(inputs),
+        out_specs=[VMEM] * len(out) if isinstance(out, (list, tuple)) else VMEM,
         scratch_shapes=list(scratch),
         cost_estimate=pl.CostEstimate(flops=flops, bytes_accessed=1 << 20, transcendentals=0),
-        compiler_params=pltpu.CompilerParams(vmem_limit_bytes=32 << 20),
+        compiler_params=pltpu.CompilerParams(vmem_limit_bytes=16 << 20),
     )(*inputs)
 
 
@@ -53,21 +59,40 @@
 
 
 def one_hot(low):
-    return jnp.where(iota((LANES, LANES), 0) == low, 1.0, 0.0).astype(jnp.bfloat16)
-
-
-def looked_up(table, highs, columns, start):
+    place = iota((LANES, LANES), 0).astype(jnp.float32).astype(jnp.bfloat16)
+    low = jnp.broadcast_to(low.astype(jnp.float32).astype(jnp.bfloat16), (LANES, LANES))
+    return jnp.where(place == low, jnp.ones((), jnp.bfloat16), jnp.zeros((), jnp.bfloat16))
+
+
+def looked_up(table, fields, highs, columns):
     products = jnp.dot(
         table, jnp.concatenate([columns, columns], 0), preferred_element_type=jnp.float32
     )
+    rows = table.shape[0] // fields
+    place = iota((8, LANES), 0)
     found = []
     for i, high in enumerate(highs):
-        total = jnp.full((8, LANES), start, jnp.float32)
-        for row in range(table.shape[0] // 8):
-            part = products[8 * row : 8 * row + 8, LANES * i : LANES * (i + 1)]
-            total = jnp.where(high == row, part, total)
-        found.append(total)
+        lanes = slice(LANES * i, LANES * (i + 1))
+        named = [place == high - 8 * g for g in range(rows // 8)]
+        values = []
+        for f in range(fields):
+            total = jnp.zeros((8, LANES), jnp.float32)
+            for g, here in enumerate(named):
+                start = rows * f + 8 * g
+                total = jnp.where(here, products[start : start + 8, lanes], total)
+            for shift in (4, 2, 1):
+                total = total + pltpu.roll(total, shift, 0)
+            values.append(total)
+        found.append(values)
     return found
+
+
+def stacked(values):
+    place = iota((8, LANES), 0)
+    tile = values[0]
+    for f in range(1, len(values)):
+        tile = jnp.where(place == f, values[f], tile)
+    return tile
 
 
 def spread(row):
@@ -81,29 +106,40 @@
     return block.T
 
 
-def first_layer_kernel(disp_ref, out_ref):
-    out_ref[...] = transposed_lanes(disp_ref[...])[0:8]
-
-
-def route_kernel(owners, helper_ref, source_ref, target_ref, member_ref, ranks_ref):
+def fetch_kernel(count, *refs):
+    inputs, (first_ref, *kept, sems) = refs[:count], refs[count:]
+    copies = [
+        pltpu.make_async_copy(source, target, sems.at[i])
+        for i, (source, target) in enumerate(zip(inputs, kept))
+    ]
+    for copy in copies:
+        copy.start()
+    copies[0].wait()
+    first_ref[...] = transposed_lanes(kept[0][...])[0:8]
+    for copy in copies[1:]:
+        copy.wait()
+
+
+def route_kernel(
+    owners, helper_ref, weights_hbm, high_ref, low_ref, rank_ref, weights_ref, member_ref, ranks_ref, sem
+):
+    copy = pltpu.make_async_copy(weights_hbm, weights_ref, sem)
+    copy.start()
     blocks = helper_ref.shape[0]
     upper = (iota((LANES, 2 * LANES), 0) <= iota((LANES, 2 * LANES), 1)).astype(jnp.bfloat16)
     owner = iota((owners, LANES), 0)
     lane = iota((owners, LANES), 1)
-    place = iota((LANES, LANES), 0)
     before = jnp.zeros((owners, LANES), jnp.float32)
     for block in range(blocks):
-        helper = helper_ref[pl.ds(block, 1), :]
-        member = helper == owner
+        member = helper_ref[pl.ds(block, 1), :] == owner
         counted = jnp.dot(
             jnp.where(member, 1.0, 0.0).astype(jnp.bfloat16),
             upper,
             preferred_element_type=jnp.float32,
         )
         rank = before + counted[:, :LANES] - 1.0
-        rank = jnp.sum(jnp.where(member, rank, 0.0), 0, keepdims=True).astype(jnp.int32)
+        rank = jnp.sum(jnp.where(member, rank, 0.0), 0, keepdims=True)
         before = before + counted[:, LANES:]
-        target_ref[pl.ds(block, 1), :] = helper * LANES + rank
         columns = pl.ds(block * LANES, LANES)
         member_ref[pl.ds(0, owners), columns] = jnp.where(member, float(block), 0.0).astype(
             jnp.bfloat16
@@ -111,11 +147,16 @@
         member_ref[pl.ds(owners, owners), columns] = jnp.where(
             member, (lane + 1).astype(jnp.float32), 0.0
         ).astype(jnp.bfloat16)
-        ranks_ref[:, columns] = jnp.where(place == rank, 1.0, 0.0).astype(jnp.bfloat16)
+        rank_ref[pl.ds(block, 1), :] = rank
+        ranks_ref[:, columns] = one_hot(rank)
     found = lax.dot_general(
         member_ref[...], ranks_ref[...], NT, preferred_element_type=jnp.float32
     ).astype(jnp.int32)
-    source_ref[...] = found[:owners] * LANES + found[owners:] - 1
+    lows = found[owners:] - 1
+    high_ref[...] = jnp.where(lows < 0, -1, found[:owners])
+    for bucket in range(owners):
+        low_ref[:, pl.ds(bucket * LANES, LANES)] = one_hot(lows[bucket : bucket + 1])
+    copy.wait()
 
 
 def strain_kernel(
@@ -126,7 +167,8 @@
     first_ref,
     side_ref,
     next_ref,
-    source_ref,
+    high_ref,
+    low_ref,
     slot_ref,
     out_ref,
     field_ref,
@@ -172,7 +214,7 @@
         grad_x = [0.25 * (sums[c, x + 1][0] - sums[c, x][0]) for c in range(3)]
         grad_y = [0.25 * (sums[c, x + 1][1] + sums[c, x][1]) for c in range(3)]
         grad_z = [0.25 * (sums[c, x + 1][2] + sums[c, x][2]) for c in range(3)]
-        slot = slot_ref[pl.ds(8 * x, 8), :].astype(jnp.float32)
+        slot = (slot_ref[pl.ds(8 * x, 8), :] + 1).astype(jnp.float32)
         fields = (
             grad_x[0],
             grad_y[1],
@@ -181,37 +223,33 @@
             grad_z[0] + grad_x[2],
             grad_y[0] + grad_x[1],
             slot,
-            slot,
         )
         for f, field in enumerate(fields):
-            field_ref[pl.ds(64 * x + f, 8, stride=8), :] = field
+            field_ref[pl.ds(8 * (planes * f + x), 8), :] = field
     table = halves(field_ref[...])
     for owner in range(0, owners, STEP):
-        rows = [source_ref[pl.ds(o, 1), :] for o in range(owner, owner + STEP)]
-        columns = jnp.concatenate([one_hot(row & (LANES - 1)) for row in rows], 1)
-        found = looked_up(table, [spread(row >> 7) for row in rows], columns, -1.0)
-        for i in range(STEP):
-            out_ref[owner + i] = found[i]
-
-
-def tangent_kernel(weights_ref, class_ref, blocks_ref, matrix_ref, out_ref):
-    points = weights_ref.shape[0]
+        steps = range(owner, owner + STEP)
+        highs = [spread(high_ref[pl.ds(o, 1), :]) for o in steps]
+        columns = low_ref[:, pl.ds(owner * LANES, STEP * LANES)]
+        for o, found in zip(steps, looked_up(table, 7, highs, columns)):
+            out_ref[pl.ds(7 * o, 7), :] = stacked(found)[0:7]
+
+
+def tangent_kernel(weights_ref, class_ref, blocks_ref, matrix_ref, out_ref, square_ref):
     fibres = blocks_ref[...].astype(jnp.float32)
     gap = jnp.zeros((2, fibres.shape[1]), jnp.float32)
     pieces = []
     for m in range(6):
         pieces += [fibres[6 * m : 6 * m + 6], gap]
     fibres = jnp.concatenate(pieces, 0).astype(jnp.bfloat16)
-    row = iota((8, LANES), 0)
-    matrix = []
-    for m in range(6):
-        column = jnp.zeros((8, LANES), jnp.float32)
-        for n in range(6):
-            column = jnp.where(row == n, matrix_ref[m, n], column)
-        matrix.append(column)
-    matrix = jnp.concatenate(matrix, 0)
+    square_ref[...] = jnp.zeros(square_ref.shape, jnp.float32)
+    square_ref[0:6, 0:6] = matrix_ref[...]
+    turned = transposed_lanes(square_ref[...])
+    matrix = jnp.concatenate(
+        [jnp.broadcast_to(turned[0:8, m : m + 1], (8, LANES)) for m in range(6)], 0
+    )
     chunk = 1024
-    for start in range(0, points, chunk):
+    for start in range(0, out_ref.shape[1], chunk):
         parts = []
         for group in range(CLASSES):
             columns = slice(LANES * group, LANES * (group + 1))
@@ -233,14 +271,23 @@
             out_ref[:, pl.ds(start + LANES * block, LANES)] = total * scale + matrix
 
 
-def respond_kernel(arrived_ref, tangent_ref, out_ref, member_ref, lows_ref, answer_ref):
-    owners = arrived_ref.shape[0]
+def fields_first(packed_ref, width):
+    rows = packed_ref.shape[0] // width
+    return halves(
+        jnp.concatenate([packed_ref[pl.ds(f, rows, stride=width), :] for f in range(6)], 0)
+    )
+
+
+def respond_kernel(
+    arrived_ref, tangent_ref, out_ref, member_ref, lows_ref, answer_ref
+):
+    owners = arrived_ref.shape[0] // 7
     blocks = tangent_ref.shape[1] // LANES
     rows = iota((blocks, LANES), 0)
     lane = (iota((blocks, LANES), 1) + 1).astype(jnp.float32)
     slots = []
     for sender in range(owners):
-        slot = arrived_ref[sender, 6:7, :].astype(jnp.int32)
+        slot = arrived_ref[pl.ds(7 * sender + 6, 1), :].astype(jnp.int32) - 1
         slots.append(slot)
         named = rows == (slot >> 7)
         columns = pl.ds(sender * LANES, LANES)
@@ -253,39 +300,36 @@
         member_ref[...], lows_ref[...], NT, preferred_element_type=jnp.float32
     ).astype(jnp.int32)
 
-    table = halves(arrived_ref[...].reshape(8 * owners, LANES))
+    table = fields_first(arrived_ref, 7)
     for block in range(0, blocks, STEP):
         steps = range(block, block + STEP)
         columns = jnp.concatenate([one_hot(where[blocks + b : blocks + b + 1] - 1) for b in steps], 1)
-        found = looked_up(table, [spread(where[b : b + 1]) for b in steps], columns, 0.0)
+        found = looked_up(table, 6, [spread(where[b : b + 1]) for b in steps], columns)
         for i, b in enumerate(steps):
+            lanes = pl.ds(b * LANES, LANES)
             total = jnp.zeros((8, LANES), jnp.float32)
             for m in range(6):
-                tangent = tangent_ref[pl.ds(8 * m, 8), pl.ds(b * LANES, LANES)]
-                total = total + tangent * spread(found[i][m : m + 1])
+                total = total + tangent_ref[pl.ds(8 * m, 8), lanes] * found[i][m]
             answer_ref[pl.ds(8 * b, 8), :] = total
 
-    table = halves(answer_ref[...])
+    table = fields_first(answer_ref, 8)
     for sender in range(0, owners, STEP):
         columns = lows_ref[:, pl.ds(sender * LANES, STEP * LANES)]
         highs = [spread(slot >> 7) for slot in slots[sender : sender + STEP]]
-        found = looked_up(table, highs, columns, 0.0)
-        for i in range(STEP):
-            out_ref[sender + i] = found[i]
-
-
-def collect_kernel(returned_ref, target_ref, sens_ref, last_ref, point_ref):
-    owners = returned_ref.shape[0]
-    blocks = target_ref.shape[0]
-    table = halves(returned_ref[...].reshape(8 * owners, LANES))
+        for i, found in enumerate(looked_up(table, 6, highs, columns)):
+            out_ref[pl.ds(6 * (sender + i), 6), :] = stacked(found)[0:6]
+
+
+def collect_kernel(returned_ref, helper_ref, rank_ref, sens_ref, last_ref):
+    blocks = helper_ref.shape[0]
+    table = fields_first(returned_ref, 6)
     for block in range(0, blocks, STEP):
-        rows = [target_ref[pl.ds(b, 1), :] for b in range(block, block + STEP)]
-        columns = jnp.concatenate([one_hot(row & (LANES - 1)) for row in rows], 1)
-        found = looked_up(table, [spread(row >> 7) for row in rows], columns, 0.0)
-        for i in range(STEP):
-            point_ref[pl.ds(8 * (block + i), 8), :] = found[i]
-    for f in range(6):
-        sens_ref[pl.ds(blocks * f, blocks), :] = point_ref[pl.ds(f, blocks, stride=8), :]
+        steps = range(block, block + STEP)
+        highs = [spread(helper_ref[pl.ds(b, 1), :]) for b in steps]
+        columns = jnp.concatenate([one_hot(rank_ref[pl.ds(b, 1), :]) for b in steps], 1)
+        for i, found in enumerate(looked_up(table, 6, highs, columns)):
+            for f in range(6):
+                sens_ref[pl.ds(blocks * f + block + i, 1), :] = found[f][0:1]
     half = 3 * blocks
     for part in range(2):
         turned = transposed_lanes(sens_ref[pl.ds(half * part, half), :])
@@ -352,24 +396,71 @@
     points = width_x * width_y * width_z
     blocks = points // LANES
     fibres = fibre_weights.shape[1]
-    disp = adjoint_disp.reshape(3 * blocks, LANES)
-    helper = rve_helper.reshape(blocks, LANES)
-    slot = rve_slot.reshape(blocks, LANES)
-
     places = [lax.axis_index(axis) for axis in ("gx", "gy", "gz")]
     ends = [lax.axis_size(axis) - 1 for axis in ("gx", "gy", "gz")]
     inside = jnp.stack(
         [place < end for place, end in zip(places, ends)] + [place > 0 for place in places]
     ).astype(jnp.int32)
 
+    with jax.named_scope("fetch"):
+        inputs = (
+            adjoint_disp.reshape(3 * blocks, LANES),
+            rve_helper.reshape(blocks, LANES),
+            rve_slot.reshape(blocks, LANES),
+            rve_class.reshape(blocks, LANES),
+            fibre_blocks,
+            matrix_tangent,
+        )
+        kept = [jax.ShapeDtypeStruct(a.shape, a.dtype) for a in inputs]
+        first, disp, helper, slot, level, fibre, matrix = whole_call(
+            functools.partial(fetch_kernel, len(inputs)),
+            "fetch",
+            [f32(8, LANES)] + kept,
+            [pltpu.with_memory_space_constraint(a, pltpu.HBM) for a in inputs],
+            [pltpu.SemaphoreType.DMA((len(inputs),))],
+            places=[HBM] * len(inputs),
+        )
+        disp_grid = disp.reshape(3, width_x, width_y, LANES)
+
+    with jax.named_scope("route"):
+        high, low, rank, weights = whole_call(
+            functools.partial(route_kernel, owners),
+            "route",
+            [
+                i32(owners, LANES),
+                jax.ShapeDtypeStruct((LANES, owners * LANES), jnp.bfloat16),
+                f32(blocks, LANES),
+                jax.ShapeDtypeStruct(fibre_weights.shape, fibre_weights.dtype),
+            ],
+            (helper, pltpu.with_memory_space_constraint(fibre_weights, pltpu.HBM)),
+            [
+                pltpu.VMEM((2 * owners, points), jnp.bfloat16),
+                pltpu.VMEM((LANES, points), jnp.bfloat16),
+                pltpu.SemaphoreType.DMA(()),
+            ],
+            flops=2 * points * LANES * 2 * owners,
+            places=[VMEM, HBM],
+        )
+
+    with jax.named_scope("tangent"):
+        tangent = whole_call(
+            tangent_kernel,
+            "tangent",
+            f32(48, points),
+            (weights, level, fibre, matrix),
+            [pltpu.VMEM((8, LANES), jnp.float32)],
+            flops=2 * 256 * points * fibres,
+        )
+
     with jax.named_scope("lift"):
-        first = whole_call(first_layer_kernel, "first_layer", f32(8, LANES), (disp,))
         first = passed_round(first, "gz", -1)
-        side = jnp.concatenate([adjoint_disp[:, 0].reshape(24, LANES), first], 0)
+        first, high, low, rank = lax.optimization_barrier((first, high, low, rank))
+        side = jnp.concatenate([disp_grid[:, 0].reshape(24, LANES), first], 0)
         side = passed_round(side, "gx", -1)
+        side, tangent = lax.optimization_barrier((side, tangent))
         next_y = jnp.concatenate(
             [
-                adjoint_disp[:, :, 0].reshape(3 * width_x, LANES),
+                disp_grid[:, :, 0].reshape(3 * width_x, LANES),
                 side[0:24:8],
                 first[0:1],
                 side[24:25],
@@ -378,47 +469,24 @@
         )
         next_y = passed_round(next_y, "gy", -1)
 
-    with jax.named_scope("route"):
-        source, target = whole_call(
-            functools.partial(route_kernel, owners),
-            "route",
-            [i32(owners, LANES), i32(blocks, LANES)],
-            (helper,),
-            [
-                pltpu.VMEM((2 * owners, points), jnp.bfloat16),
-                pltpu.VMEM((LANES, points), jnp.bfloat16),
-            ],
-            flops=2 * points * LANES * 2 * owners,
-        )
-
     with jax.named_scope("strain"):
         buckets = whole_call(
             functools.partial(strain_kernel, owners, width_x),
             "strain",
-            f32(owners, 8, LANES),
-            (inside, disp, first, side, next_y, source, slot),
-            [pltpu.VMEM((8 * blocks, LANES), jnp.float32)],
-            scalars=(0,),
-        )
-
-    with jax.named_scope("tangent"):
-        tangent = whole_call(
-            tangent_kernel,
-            "tangent",
-            f32(48, points),
-            (fibre_weights, rve_class.reshape(blocks, LANES), fibre_blocks, matrix_tangent),
-            flops=2 * 256 * points * fibres,
-            scalars=(3,),
+            f32(owners * 7, LANES),
+            (inside, disp, first, side, next_y, high, low, slot),
+            [pltpu.VMEM((7 * blocks, LANES), jnp.float32)],
+            places=[SMEM] + [VMEM] * 7,
         )
 
     with jax.named_scope("exchange"):
-        arrived = lax.all_to_all(buckets, ("gx", "gy"), split_axis=0, concat_axis=0, tiled=True)
+        arrived = exchanged(buckets, owners, ("gx", "gy"))
 
     with jax.named_scope("respond"):
         answer = whole_call(
             respond_kernel,
             "respond",
-            f32(owners, 8, LANES),
+            f32(owners * 6, LANES),
             (arrived, tangent),
             [
                 pltpu.VMEM((2 * blocks, owners * LANES), jnp.bfloat16),
@@ -428,15 +496,14 @@
         )
 
     with jax.named_scope("return"):
-        returned = lax.all_to_all(answer, ("gx", "gy"), split_axis=0, concat_axis=0, tiled=True)
+        returned = exchanged(answer, owners, ("gx", "gy"))
 
     with jax.named_scope("collect"):
         sens, last = whole_call(
             collect_kernel,
             "collect",
             [f32(6 * blocks, LANES), f32(8, LANES)],
-            (returned, target),
-            [pltpu.VMEM((8 * blocks, LANES), jnp.float32)],
+            (returned, helper, rank),
         )
 
     with jax.named_scope("settle"):
@@ -459,7 +526,7 @@
             "force",
             f32(3 * blocks, LANES),
             (inside, sens, last, side, prior),
-            scalars=(0,),
+            places=[SMEM] + [VMEM] * 4,
         )
     return force.reshape(3, width_x, width_y, width_z)
 

time: 80.3 us -> 74.5 us (0.928)
  blocking collectives: 17.7 us -> 37 us
  waiting for transfers between devices: 24 us -> 14.5 us
  local copies, waits for them, and re-layouts: 7.59 us -> 0.18 us
  starting transfers between devices: 16.6 us -> 9.58 us
  Pallas kernels: 13.8 us -> 12.9 us
    all_to_all x1 -> x2, blocking collectives: 17.7 us -> 37 us  [exchanged(): flat = lax.all_to_all(flat, axes, split_axis=0, concat_axis=0, tiled=True)]
    all_to_all x1 -> x0, starting transfers between devices: 8.58 us -> none  [per_device(): lax.all_to_all(buckets, ('gx', 'gy'), split_axis=0, concat_axis=0, tiled=...]
    unnamed x16 -> x0, local copies, waits for them, and re-layouts: 7.39 us -> none
    all_to_all x1 -> x0, waiting for transfers between devices: 6.42 us -> none  [per_device(): lax.all_to_all(buckets, ('gx', 'gy'), split_axis=0, concat_axis=0, tiled=...]
    ppermute x6, waiting for transfers between devices: 17.5 us -> 14.5 us  [passed_round(): lax.ppermute(array, axis, [(i, (i + by) % devices) for i in range(devices)])]
    ppermute x6, starting transfers between devices: 8.05 us -> 9.58 us  [passed_round(): lax.ppermute(array, axis, [(i, (i + by) % devices) for i in range(devices)])]
    pallas_call x7, Pallas kernels: 13.8 us -> 12.9 us  [whole_call(): pl.pallas_call(kernel, name=name, out_shape=out, in_specs=places or [VMEM...]
  transfers between devices with their start and end apart: 7 -> 6, of which waited for: 6 -> 5; matrix products, arithmetic and copies ran while one was open for 0% -> 0% of each run, Pallas kernels for 4% -> 5%
where the time goes in v2:
time: 74.5 us; the launch traced here: 74.3 us
  blocking collectives  37 us (50%)
  waiting for transfers between devices  14.5 us (19%)
  Pallas kernels  12.9 us (17%)
  starting transfers between devices  9.58 us (13%)
    all_to_all x2, blocking collectives, exchanged(): flat = lax.all_to_all(flat, axes, split_axis=0, concat_axis=0, tiled=True)  37 us
    ppermute x6, waiting for transfers between devices, passed_round(): lax.ppermute(array, axis, [(i, (i + by) % devices) for i in range(devices)])  14.5 us
    pallas_call x7, Pallas kernels, whole_call(): pl.pallas_call(kernel, name=name, out_shape=out, in_specs=places or [VMEM...  12.9 us
    ppermute x6, starting transfers between devices, passed_round(): lax.ppermute(array, axis, [(i, (i + by) % devices) for i in range(devices)])  9.58 us
  transfers between devices with their start and end apart: 6, of which 5 were waited for; matrix products, arithmetic and copies ran while one was open for 0% of the time, Pallas kernels for 5%

profile of v2, /device:TPU:6, one launch (start us, length us, event | category | flops | bytes accessed | tf_op | source)
XLA Modules:
  0.0 74.3 jit_solution(5319583577560268129)
XLA Ops:
  0.0 0.9 %fetch.1 = (f32[8,128]{1,0:T(8,128)S(1)}, f32[96,128]{1,0:T(8,128)S(1)}, s32[32,128]{1,0:T(8,128)S(1)}, s32[32,128]{1,0:T(8,128)S(1)}, s32[32,128]{1,0:T(8,128)S...) custom-call(f32[96,128]{1,0:T(8,128)} %bitcast.40, s32[32,128]{1,0:T(8,128)} %bitcast.42, s32[32,128]{1,0:T(8,128)} %bitcast.43, ...), custom_call_target="tpu_custom_call" | custom-call | bytes 1048576 | tf_op jit(solution)/shard_map/fetch/fetch/pallas_call | solution.py:31
  0.9 0.9 %collective-permute-start = (f32[8,128]{1,0:T(8,128)S(1)}, f32[8,128]{1,0:T(8,128)S(1)}, u32[]{:S(2)}, u32[]{:S(2)}) collective-permute-start(f32[8,128]{1,0:T(8,128)S(1)} %get-tuple-element.25), channel_id=1, source_target_pairs={{0,3},{1,0},{2,1},{3,2},{4,7},{5,4},{6,5},{7,6},{8,11},{9,8},{10,9... | collective-permute-start | bytes 12296 | tf_op jit(solution)/shard_map/lift/ppermute | solution.py:21
  1.8 2.2 %route.1 = (s32[64,128]{1,0:T(8,128)S(1)}, bf16[128,8192]{1,0:T(8,128)(2,1)S(1)}, f32[32,128]{1,0:T(8,128)S(1)}, bf16[4096,512]{1,0:T(8,128)(2,1)S(1)}) custom-call(s32[32,128]{1,0:T(8,128)S(1)} %get-tuple-element.26.helper_ref, bf16[4096,512]{1,0:T(8,128)(2,1)} %weights_hbm.1), custom_call_target="tpu_custom_call" | custom-call | flops 134217728 | bytes 1048576 | tf_op jit(solution)/shard_map/route/route/pallas_call | solution.py:31
  4.1 1.8 %collective-permute-done.first_ref = f32[8,128]{1,0:T(8,128)S(1)} collective-permute-done((f32[8,128]{1,0:T(8,128)S(1)}, f32[8,128]{1,0:T(8,128)S(1)}, u32[]{:S(2)}, u32[]{:S(2)}) %collective-permute-start) | collective-permute-done | bytes 4128 | tf_op jit(solution)/shard_map/lift/ppermute | solution.py:21
  5.8 5.9 %collective-permute-start.1 = (f32[32,128]{1,0:T(8,128)S(1)}, f32[32,128]{1,0:T(8,128)S(1)}, u32[]{:S(2)}, u32[]{:S(2)}) collective-permute-start(f32[32,128]{1,0:T(8,128)S(1)} %pad_maximum_fusion.2), channel_id=1, source_target_pairs={{0,224},{32,0},{64,32},{96,64},{128,96},{160,128},{192,160},{224,1... | collective-permute-start | bytes 49160 | tf_op jit(solution)/shard_map/lift/ppermute | solution.py:21
  11.7 1.6 %tangent.1.tangent_ref = f32[48,4096]{1,0:T(8,128)S(1)} custom-call(bf16[4096,512]{1,0:T(8,128)(2,1)S(1)} %get-tuple-element.31.weights_ref, s32[32,128]{1,0:T(8,128)S(1)} %get-tuple-element.32.class_ref, bf16[36,512]{1,0:T(8,128)(2,1)S(1)} %get-tuple-element.33.blocks_ref, f32[6,6]{1,0:T(8,128)S(1)} %get-tuple-element.34.matrix_ref), custom_call_target="tpu_custom_call" | custom-call | flops 1073741824 | bytes 1048576 | tf_op jit(solution)/shard_map/tangent/tangent/pallas_call | solution.py:31
  13.3 0.0 collective-permute-done.1.side_ref
  13.4 1.0 %collective-permute-start.2 = (f32[17,128]{1,0:T(8,128)S(1)}, f32[17,128]{1,0:T(8,128)S(1)}, u32[]{:S(2)}, u32[]{:S(2)}) collective-permute-start(f32[17,128]{1,0:T(8,128)S(1)} %pad_maximum_fusion.3), channel_id=1, source_target_pairs={{0,28},{4,0},{8,4},{12,8},{16,12},{20,16},{24,20},{28,24},{1,29},{... | collective-permute-start | bytes 26120 | tf_op jit(solution)/shard_map/lift/ppermute | solution.py:21
  14.4 0.1 stack.27
  14.5 1.3 %collective-permute-done.2.next_ref = f32[17,128]{1,0:T(8,128)S(1)} collective-permute-done((f32[17,128]{1,0:T(8,128)S(1)}, f32[17,128]{1,0:T(8,128)S(1)}, u32[]{:S(2)}, u32[]{:S(2)}) %collective-permute-start.2) | collective-permute-done | bytes 8736 | tf_op jit(solution)/shard_map/lift/ppermute | solution.py:21
  15.8 1.8 %strain.1 = f32[448,128]{1,0:T(8,128)S(1)} custom-call(s32[6]{0:T(128)S(1)} %convert_element_type.3.inside_ref, f32[96,128]{1,0:T(8,128)S(1)} %get-tuple-element.24.disp_ref, f32[8,128]{1,0:T(8,128)S(1)} %collective-permute-done.first_ref, f32[32,128]{1,0:T(8,128)S(1)} %collective-permute-done.1.side_ref, f32[17,128]{1,0:T(8,128)S(1)} %collective-permute-done.2.next_ref, ...), custom_call_target="tpu_custom_call" | custom-call | bytes 1048576 | tf_op jit(solution)/shard_map/strain/strain/pallas_call | solution.py:31
  17.7 20.5 %all_to_all.10 = f32[64,1,896]{2,1,0:T(1,128)S(1)} all-to-all(f32[64,1,896]{2,1,0:T(1,128)S(1)} %bitcast.32), channel_id=1, replica_groups=mesh['gx'=8,'gy'=8,'gz'=4] {'gx','gy'}, dimensions={0} | all-to-all | bytes 458752 | tf_op jit(solution)/shard_map/exchange/all_to_all | solution.py:26
  38.2 3.9 %respond.1 = f32[384,128]{1,0:T(8,128)S(1)} custom-call(f32[448,128]{1,0:T(8,128)S(1)} %bitcast.31, f32[48,4096]{1,0:T(8,128)S(1)} %tangent.1.tangent_ref), custom_call_target="tpu_custom_call" | custom-call | bytes 1048576 | tf_op jit(solution)/shard_map/respond/respond/pallas_call | solution.py:31
  42.0 16.5 %all_to_all.11 = f32[64,1,768]{2,1,0:T(1,128)S(1)} all-to-all(f32[64,1,768]{2,1,0:T(1,128)S(1)} %bitcast.33), channel_id=1, replica_groups=mesh['gx'=8,'gy'=8,'gz'=4] {'gx','gy'}, dimensions={0} | all-to-all | bytes 393216 | tf_op jit(solution)/shard_map/return/all_to_all | solution.py:26
  58.6 1.1 %collect.1 = (f32[192,128]{1,0:T(8,128)S(1)}, f32[8,128]{1,0:T(8,128)S(1)}) custom-call(f32[384,128]{1,0:T(8,128)S(1)} %bitcast.34, s32[32,128]{1,0:T(8,128)S(1)} %get-tuple-element.26.helper_ref, f32[32,128]{1,0:T(8,128)S(1)} %get-tuple-element.40.rank_ref), custom_call_target="tpu_custom_call" | custom-call | bytes 1048576 | tf_op jit(solution)/shard_map/collect/collect/pallas_call | solution.py:31
  59.6 0.8 %collective-permute-start.3 = (f32[8,128]{1,0:T(8,128)S(1)}, f32[8,128]{1,0:T(8,128)S(1)}, u32[]{:S(2)}, u32[]{:S(2)}) collective-permute-start(f32[8,128]{1,0:T(8,128)S(1)} %get-tuple-element.42), channel_id=1, source_target_pairs={{0,1},{1,2},{2,3},{3,0},{4,5},{5,6},{6,7},{7,4},{8,9},{9,10},{10,1... | collective-permute-start | bytes 12296 | tf_op jit(solution)/shard_map/settle/ppermute | solution.py:21
  60.5 2.9 %collective-permute-done.3.last_ref = f32[8,128]{1,0:T(8,128)S(1)} collective-permute-done((f32[8,128]{1,0:T(8,128)S(1)}, f32[8,128]{1,0:T(8,128)S(1)}, u32[]{:S(2)}, u32[]{:S(2)}) %collective-permute-start.3) | collective-permute-done | bytes 4128 | tf_op jit(solution)/shard_map/settle/ppermute | solution.py:21
  63.3 1.0 %collective-permute-start.4 = (f32[56,128]{1,0:T(8,128)S(1)}, f32[56,128]{1,0:T(8,128)S(1)}, u32[]{:S(2)}, u32[]{:S(2)}) collective-permute-start(f32[56,128]{1,0:T(8,128)S(1)} %pad_maximum_fusion), channel_id=1, source_target_pairs={{0,32},{32,64},{64,96},{96,128},{128,160},{160,192},{192,224},{224... | collective-permute-start | bytes 86024 | tf_op jit(solution)/shard_map/settle/ppermute | solution.py:21
  64.3 4.1 %collective-permute-done.4.side_ref = f32[56,128]{1,0:T(8,128)S(1)} collective-permute-done((f32[56,128]{1,0:T(8,128)S(1)}, f32[56,128]{1,0:T(8,128)S(1)}, u32[]{:S(2)}, u32[]{:S(2)}) %collective-permute-start.4) | collective-permute-done | bytes 28704 | tf_op jit(solution)/shard_map/settle/ppermute | solution.py:21
  68.5 0.0 collective-permute-start.5
  68.5 4.4 %collective-permute-done.5.prior_ref = f32[34,128]{1,0:T(8,128)S(1)} collective-permute-done((f32[34,128]{1,0:T(8,128)S(1)}, f32[34,128]{1,0:T(8,128)S(1)}, u32[]{:S(2)}, u32[]{:S(2)}) %collective-permute-start.5) | collective-permute-done | bytes 17440 | tf_op jit(solution)/shard_map/settle/ppermute | solution.py:21
  72.9 1.4 %force.1 = f32[96,128]{1,0:T(8,128)} custom-call(s32[6]{0:T(128)S(1)} %convert_element_type.3.inside_ref, f32[192,128]{1,0:T(8,128)S(1)} %get-tuple-element.41.sens_ref, f32[8,128]{1,0:T(8,128)S(1)} %collective-permute-done.3.last_ref, f32[56,128]{1,0:T(8,128)S(1)} %collective-permute-done.4.side_ref, f32[34,128]{1,0:T(8,128)S(1)} %collective-permute-done.5.prior_ref), custom_call_target="tpu_custom_call" | custom-call | bytes 1048576 | tf_op jit(solution)/shard_map/settle/force/pallas_call | solution.py:31
  (16 shorter events, 0.1 us)
Async XLA Ops:
  0.9 4.9 %collective-permute-start = (f32[8,128]{1,0:T(8,128)S(1)}, f32[8,128]{1,0:T(8,128)S(1)}, u32[]{:S(2)}, u32[]{:S(2)}) collective-permute-start(f32[8,128]{1,0:T(8,128)S(1)} %get-tuple-element.25), channel_id=1, source_target_pairs={{0,3},{1,0},{2,1},{3,2},{4,7},{5,4},{6,5},{7,6},{8,11},{9,8},{10,9... | collective-permute-start | bytes 12296 | tf_op jit(solution)/shard_map/lift/ppermute | solution.py:21
  5.8 7.5 %collective-permute-start.1 = (f32[32,128]{1,0:T(8,128)S(1)}, f32[32,128]{1,0:T(8,128)S(1)}, u32[]{:S(2)}, u32[]{:S(2)}) collective-permute-start(f32[32,128]{1,0:T(8,128)S(1)} %pad_maximum_fusion.2), channel_id=1, source_target_pairs={{0,224},{32,0},{64,32},{96,64},{128,96},{160,128},{192,160},{224,1... | collective-permute-start | bytes 49160 | tf_op jit(solution)/shard_map/lift/ppermute | solution.py:21
  13.4 2.4 %collective-permute-start.2 = (f32[17,128]{1,0:T(8,128)S(1)}, f32[17,128]{1,0:T(8,128)S(1)}, u32[]{:S(2)}, u32[]{:S(2)}) collective-permute-start(f32[17,128]{1,0:T(8,128)S(1)} %pad_maximum_fusion.3), channel_id=1, source_target_pairs={{0,28},{4,0},{8,4},{12,8},{16,12},{20,16},{24,20},{28,24},{1,29},{... | collective-permute-start | bytes 26120 | tf_op jit(solution)/shard_map/lift/ppermute | solution.py:21
  59.6 3.7 %collective-permute-start.3 = (f32[8,128]{1,0:T(8,128)S(1)}, f32[8,128]{1,0:T(8,128)S(1)}, u32[]{:S(2)}, u32[]{:S(2)}) collective-permute-start(f32[8,128]{1,0:T(8,128)S(1)} %get-tuple-element.42), channel_id=1, source_target_pairs={{0,1},{1,2},{2,3},{3,0},{4,5},{5,6},{6,7},{7,4},{8,9},{9,10},{10,1... | collective-permute-start | bytes 12296 | tf_op jit(solution)/shard_map/settle/ppermute | solution.py:21
  63.3 5.1 %collective-permute-start.4 = (f32[56,128]{1,0:T(8,128)S(1)}, f32[56,128]{1,0:T(8,128)S(1)}, u32[]{:S(2)}, u32[]{:S(2)}) collective-permute-start(f32[56,128]{1,0:T(8,128)S(1)} %pad_maximum_fusion), channel_id=1, source_target_pairs={{0,32},{32,64},{64,96},{96,128},{128,160},{160,192},{192,224},{224... | collective-permute-start | bytes 86024 | tf_op jit(solution)/shard_map/settle/ppermute | solution.py:21
  68.5 4.4 %collective-permute-start.5 = (f32[34,128]{1,0:T(8,128)S(1)}, f32[34,128]{1,0:T(8,128)S(1)}, u32[]{:S(2)}, u32[]{:S(2)}) collective-permute-start(f32[34,128]{1,0:T(8,128)S(1)} %pad_maximum_fusion.1), channel_id=1, source_target_pairs={{0,4},{4,8},{8,12},{12,16},{16,20},{20,24},{24,28},{28,0},{1,5},{5... | collective-permute-start | bytes 52232 | tf_op jit(solution)/shard_map/settle/ppermute | solution.py:21

commit v3 on v2

--- a/solution.py
+++ b/solution.py
@@ -16,9 +16,29 @@
 NT = (((1,), (1,)), ((), ()))
 
 
-def passed_round(array, axis, by):
-    devices = lax.axis_size(axis)
-    return lax.ppermute(array, axis, [(i, (i + by) % devices) for i in range(devices)])
+def passed_round(array, axes, by):
+    pairs = [(0, 0)]
+    for axis in axes:
+        size = lax.axis_size(axis)
+        pairs = [
+            (source * size + i, target * size + (i + by) % size)
+            for source, target in pairs
+            for i in range(size)
+        ]
+    return lax.ppermute(array, axes, pairs)
+
+
+def passed_on(array, axes, by):
+    pairs = [(0, 0)]
+    for axis in axes:
+        size = lax.axis_size(axis)
+        pairs = [
+            (source * size + i, target * size + i + by)
+            for source, target in pairs
+            for i in range(size)
+            if 0 <= i + by < size
+        ]
+    return lax.ppermute(array, axes, pairs)
 
 
 def exchanged(array, owners, axes):
@@ -123,7 +143,7 @@
 def route_kernel(
     owners, helper_ref, weights_hbm, high_ref, low_ref, rank_ref, weights_ref, member_ref, ranks_ref, sem
 ):
-    copy = pltpu.make_async_copy(weights_hbm, weights_ref, sem)
+    copy = pltpu.make_async_copy(weights_hbm.at[pl.ds(0, weights_ref.shape[0])], weights_ref, sem)
     copy.start()
     blocks = helper_ref.shape[0]
     upper = (iota((LANES, 2 * LANES), 0) <= iota((LANES, 2 * LANES), 1)).astype(jnp.bfloat16)
@@ -166,6 +186,7 @@
     disp_ref,
     first_ref,
     side_ref,
+    corner_ref,
     next_ref,
     high_ref,
     low_ref,
@@ -179,7 +200,7 @@
         jnp.concatenate(
             [
                 first_ref[0:1],
-                side_ref[24:25],
+                corner_ref[0:1],
                 next_ref[15:16],
                 next_ref[16:17],
                 jnp.zeros((4, LANES), jnp.float32),
@@ -235,7 +256,28 @@
             out_ref[pl.ds(7 * o, 7), :] = stacked(found)[0:7]
 
 
-def tangent_kernel(weights_ref, class_ref, blocks_ref, matrix_ref, out_ref, square_ref):
+def tangent_kernel(first, weights_ref, class_ref, blocks_ref, matrix_ref, out_ref, square_ref):
+    tangents(first, weights_ref, [], class_ref, blocks_ref, matrix_ref, out_ref, square_ref)
+
+
+def fetched_tangent_kernel(
+    first, weights_hbm, class_ref, blocks_ref, matrix_ref, out_ref, square_ref, weights_ref, sems
+):
+    chunk = weights_ref.shape[0] // sems.shape[0]
+    copies = [
+        pltpu.make_async_copy(
+            weights_hbm.at[pl.ds(first + chunk * i, chunk)],
+            weights_ref.at[pl.ds(chunk * i, chunk)],
+            sems.at[i],
+        )
+        for i in range(sems.shape[0])
+    ]
+    for copy in copies:
+        copy.start()
+    tangents(first, weights_ref, copies, class_ref, blocks_ref, matrix_ref, out_ref, square_ref)
+
+
+def tangents(first, weights_ref, copies, class_ref, blocks_ref, matrix_ref, out_ref, square_ref):
     fibres = blocks_ref[...].astype(jnp.float32)
     gap = jnp.zeros((2, fibres.shape[1]), jnp.float32)
     pieces = []
@@ -249,7 +291,9 @@
         [jnp.broadcast_to(turned[0:8, m : m + 1], (8, LANES)) for m in range(6)], 0
     )
     chunk = 1024
-    for start in range(0, out_ref.shape[1], chunk):
+    for i, start in enumerate(range(0, weights_ref.shape[0], chunk)):
+        if copies:
+            copies[i].wait()
         parts = []
         for group in range(CLASSES):
             columns = slice(LANES * group, LANES * (group + 1))
@@ -263,7 +307,7 @@
             )
         for block in range(chunk // LANES):
             lanes = slice(LANES * block, LANES * (block + 1))
-            level = class_ref[pl.ds(start // LANES + block, 1), :]
+            level = class_ref[pl.ds((first + start) // LANES + block, 1), :]
             total = parts[0][:, lanes]
             for group in range(1, CLASSES):
                 total = total + jnp.where(level >= group, parts[group][:, lanes], 0.0)
@@ -279,10 +323,11 @@
 
 
 def respond_kernel(
-    arrived_ref, tangent_ref, out_ref, member_ref, lows_ref, answer_ref
+    arrived_ref, early_ref, late_ref, out_ref, member_ref, lows_ref, answer_ref
 ):
     owners = arrived_ref.shape[0] // 7
-    blocks = tangent_ref.shape[1] // LANES
+    half = early_ref.shape[1] // LANES
+    blocks = 2 * half
     rows = iota((blocks, LANES), 0)
     lane = (iota((blocks, LANES), 1) + 1).astype(jnp.float32)
     slots = []
@@ -306,7 +351,8 @@
         columns = jnp.concatenate([one_hot(where[blocks + b : blocks + b + 1] - 1) for b in steps], 1)
         found = looked_up(table, 6, [spread(where[b : b + 1]) for b in steps], columns)
         for i, b in enumerate(steps):
-            lanes = pl.ds(b * LANES, LANES)
+            tangent_ref = early_ref if b < half else late_ref
+            lanes = pl.ds(b % half * LANES, LANES)
             total = jnp.zeros((8, LANES), jnp.float32)
             for m in range(6):
                 total = total + tangent_ref[pl.ds(8 * m, 8), lanes] * found[i][m]
@@ -337,7 +383,7 @@
     last_ref[pl.ds(2, 6), :] = jnp.zeros((6, LANES), jnp.float32)
 
 
-def force_kernel(width_x, inside_ref, sens_ref, last_ref, side_ref, prior_ref, out_ref):
+def force_kernel(width_x, inside_ref, sens_ref, last_ref, side_ref, corner_ref, prior_ref, out_ref):
     planes = width_x
     blocks = 8 * planes
     fields = 6
@@ -345,7 +391,7 @@
     rows = jnp.concatenate(
         [
             last_ref[0:2],
-            side_ref[48:50],
+            corner_ref[0:2],
             prior_ref[30:34],
         ],
         0,
@@ -423,6 +469,7 @@
         disp_grid = disp.reshape(3, width_x, width_y, LANES)
 
     with jax.named_scope("route"):
+        weights_hbm = pltpu.with_memory_space_constraint(fibre_weights, pltpu.HBM)
         high, low, rank, weights = whole_call(
             functools.partial(route_kernel, owners),
             "route",
@@ -430,9 +477,9 @@
                 i32(owners, LANES),
                 jax.ShapeDtypeStruct((LANES, owners * LANES), jnp.bfloat16),
                 f32(blocks, LANES),
-                jax.ShapeDtypeStruct(fibre_weights.shape, fibre_weights.dtype),
+                jax.ShapeDtypeStruct((points // 2, fibres), fibre_weights.dtype),
             ],
-            (helper, pltpu.with_memory_space_constraint(fibre_weights, pltpu.HBM)),
+            (helper, weights_hbm),
             [
                 pltpu.VMEM((2 * owners, points), jnp.bfloat16),
                 pltpu.VMEM((LANES, points), jnp.bfloat16),
@@ -443,40 +490,56 @@
         )
 
     with jax.named_scope("tangent"):
-        tangent = whole_call(
-            tangent_kernel,
-            "tangent",
-            f32(48, points),
+        half = points // 2
+        early = whole_call(
+            functools.partial(tangent_kernel, 0),
+            "early_tangent",
+            f32(48, half),
             (weights, level, fibre, matrix),
             [pltpu.VMEM((8, LANES), jnp.float32)],
-            flops=2 * 256 * points * fibres,
+            flops=256 * points * fibres,
+        )
+        late = whole_call(
+            functools.partial(fetched_tangent_kernel, half),
+            "late_tangent",
+            f32(48, half),
+            (weights_hbm, level, fibre, matrix),
+            [
+                pltpu.VMEM((8, LANES), jnp.float32),
+                pltpu.VMEM((half, fibres), jnp.bfloat16),
+                pltpu.SemaphoreType.DMA((2,)),
+            ],
+            flops=256 * points * fibres,
+            places=[HBM, VMEM, VMEM, VMEM],
         )
 
     with jax.named_scope("lift"):
-        first = passed_round(first, "gz", -1)
-        first, high, low, rank = lax.optimization_barrier((first, high, low, rank))
-        side = jnp.concatenate([disp_grid[:, 0].reshape(24, LANES), first], 0)
-        side = passed_round(side, "gx", -1)
-        side, tangent = lax.optimization_barrier((side, tangent))
+        side = passed_round(disp_grid[:, 0].reshape(24, LANES), ("gx",), -1)
+        corner = passed_round(first, ("gx", "gz"), -1)
+        first = passed_round(first, ("gz",), -1)
+        side, corner, first, high, low, rank, early, inside = lax.optimization_barrier(
+            (side, corner, first, high, low, rank, early, inside)
+        )
         next_y = jnp.concatenate(
             [
                 disp_grid[:, :, 0].reshape(3 * width_x, LANES),
                 side[0:24:8],
                 first[0:1],
-                side[24:25],
+                corner[0:1],
             ],
             0,
         )
-        next_y = passed_round(next_y, "gy", -1)
+        next_y = passed_round(next_y, ("gy",), -1)
+        next_y, late = lax.optimization_barrier((next_y, late))
 
     with jax.named_scope("strain"):
         buckets = whole_call(
             functools.partial(strain_kernel, owners, width_x),
             "strain",
             f32(owners * 7, LANES),
-            (inside, disp, first, side, next_y, high, low, slot),
+            (inside, disp, first, side, corner, next_y, high, low, slot),
             [pltpu.VMEM((7 * blocks, LANES), jnp.float32)],
-            places=[SMEM] + [VMEM] * 7,
+            places=[SMEM] + [VMEM] * 8,
         )
 
     with jax.named_scope("exchange"):
@@ -487,7 +550,7 @@
             respond_kernel,
             "respond",
             f32(owners * 6, LANES),
-            (arrived, tangent),
+            (arrived, early, late),
             [
                 pltpu.VMEM((2 * blocks, owners * LANES), jnp.bfloat16),
                 pltpu.VMEM((LANES, owners * LANES), jnp.bfloat16),
@@ -508,25 +571,25 @@
 
     with jax.named_scope("settle"):
         sens_grid = sens.reshape(6, width_x, width_y, LANES)
-        last = passed_round(last, "gz", 1)
-        side = jnp.concatenate([sens_grid[:, -1].reshape(48, LANES), last], 0)
-        side = passed_round(side, "gx", 1)
+        side = passed_round(sens_grid[:, -1].reshape(48, LANES), ("gx",), 1)
+        corner = passed_on(last, ("gx", "gz"), 1)
+        last = passed_round(last, ("gz",), 1)
         prior = jnp.concatenate(
             [
                 sens_grid[:, :, -1].reshape(6 * width_x, LANES),
                 side[7:48:8],
                 last[0:2],
-                side[48:50],
+                corner[0:2],
             ],
             0,
         )
-        prior = passed_round(prior, "gy", 1)
+        prior = passed_on(prior, ("gy",), 1)
         force = whole_call(
             functools.partial(force_kernel, width_x),
             "force",
             f32(3 * blocks, LANES),
-            (inside, sens, last, side, prior),
-            places=[SMEM] + [VMEM] * 4,
+            (inside, sens, last, side, corner, prior),
+            places=[SMEM] + [VMEM] * 5,
         )
     return force.reshape(3, width_x, width_y, width_z)
 

time: 74.5 us -> 71.7 us (0.962)
  the two profiles are of different devices: /device:TPU:6 before, /device:TPU:46 now
where the time goes in v3:
time: 71.7 us; the launch traced here: 71.4 us
  blocking collectives  35.4 us (49%)
  Pallas kernels  13.8 us (19%)
  starting transfers between devices  13.5 us (19%)
  waiting for transfers between devices  8.26 us (12%)
    all_to_all x2, blocking collectives, exchanged(): flat = lax.all_to_all(flat, axes, split_axis=0, concat_axis=0, tiled=True)  35.4 us
    pallas_call x8, Pallas kernels, whole_call(): pl.pallas_call(kernel, name=name, out_shape=out, in_specs=places or [VMEM...  13.8 us
    ppermute x6, starting transfers between devices, passed_round(): return lax.ppermute(array, axes, pairs)  10.3 us
    ppermute x2, waiting for transfers between devices, passed_on(): return lax.ppermute(array, axes, pairs)  8.23 us
    ppermute x2, starting transfers between devices, passed_on(): return lax.ppermute(array, axes, pairs)  3.2 us
  transfers between devices with their start and end apart: 8, of which 2 were waited for; matrix products, arithmetic and copies ran while one was open for 0% of the time, Pallas kernels for 7%

profile of v3, /device:TPU:46, one launch (start us, length us, event | category | flops | bytes accessed | tf_op | source)
XLA Modules:
  0.0 71.4 jit_solution(8624541507043884464)
XLA Ops:
  0.0 0.9 %fetch.1 = (f32[8,128]{1,0:T(8,128)S(1)}, f32[96,128]{1,0:T(8,128)S(1)}, s32[32,128]{1,0:T(8,128)S(1)}, s32[32,128]{1,0:T(8,128)S(1)}, s32[32,128]{1,0:T(8,128)S...) custom-call(f32[96,128]{1,0:T(8,128)} %bitcast.40, s32[32,128]{1,0:T(8,128)} %bitcast.42, s32[32,128]{1,0:T(8,128)} %bitcast.43, ...), custom_call_target="tpu_custom_call" | custom-call | bytes 1048576 | tf_op jit(solution)/shard_map/fetch/fetch/pallas_call | solution.py:51
  0.9 0.5 collective-permute-start.1
  1.4 0.5 collective-permute-start.2
  1.9 5.8 %collective-permute-start = (f32[24,128]{1,0:T(8,128)S(1)}, f32[24,128]{1,0:T(8,128)S(1)}, u32[]{:S(2)}, u32[]{:S(2)}) collective-permute-start(f32[24,128]{1,0:T(8,128)S(1)} %slice_bitcast_fusion.1), channel_id=1, source_target_pairs={{0,224},{32,0},{64,32},{96,64},{128,96},{160,128},{192,160},{224,1... | collective-permute-start | bytes 36872 | tf_op jit(solution)/shard_map/lift/ppermute | solution.py:28
  7.8 1.6 %route.1 = (s32[64,128]{1,0:T(8,128)S(1)}, bf16[128,8192]{1,0:T(8,128)(2,1)S(1)}, f32[32,128]{1,0:T(8,128)S(1)}, bf16[2048,512]{1,0:T(8,128)(2,1)S(1)}) custom-call(s32[32,128]{1,0:T(8,128)S(1)} %get-tuple-element.30.helper_ref, bf16[4096,512]{1,0:T(8,128)(2,1)} %weights_hbm.3), custom_call_target="tpu_custom_call" | custom-call | flops 134217728 | bytes 1048576 | tf_op jit(solution)/shard_map/route/route/pallas_call | solution.py:51
  9.4 0.8 %early_tangent.1.early_ref = f32[48,2048]{1,0:T(8,128)S(1)} custom-call(bf16[2048,512]{1,0:T(8,128)(2,1)S(1)} %get-tuple-element.34.weights_ref, s32[32,128]{1,0:T(8,128)S(1)} %get-tuple-element.35.class_ref, bf16[36,512]{1,0:T(8,128)(2,1)S(1)} %get-tuple-element.36.blocks_ref, f32[6,6]{1,0:T(8,128)S(1)} %get-tuple-element.37.matrix_ref), custom_call_target="tpu_custom_call" | custom-call | flops 536870912 | bytes 1048576 | tf_op jit(solution)/shard_map/tangent/early_tangent/pallas_call | solution.py:51
  10.3 0.1 stack.27
  10.4 0.0 collective-permute-done.1.corner_ref
  10.4 0.0 collective-permute-done.2.first_ref
  10.4 0.0 collective-permute-done.side_ref
  10.5 0.0 collective-permute-start.3
  10.5 2.2 %late_tangent.1.late_ref = f32[48,2048]{1,0:T(8,128)S(1)} custom-call(bf16[4096,512]{1,0:T(8,128)(2,1)} %weights_hbm.3, s32[32,128]{1,0:T(8,128)S(1)} %get-tuple-element.35.class_ref, bf16[36,512]{1,0:T(8,128)(2,1)S(1)} %get-tuple-element.36.blocks_ref, f32[6,6]{1,0:T(8,128)S(1)} %get-tuple-element.37.matrix_ref), custom_call_target="tpu_custom_call" | custom-call | flops 536870912 | bytes 1048576 | tf_op jit(solution)/shard_map/tangent/late_tangent/pallas_call | solution.py:51
  12.7 0.0 collective-permute-done.3.next_ref
  12.7 1.8 %strain.1 = f32[448,128]{1,0:T(8,128)S(1)} custom-call(s32[6]{0:T(128)S(1)} %convert_element_type.3.inside_ref, f32[96,128]{1,0:T(8,128)S(1)} %get-tuple-element.28.disp_ref, f32[8,128]{1,0:T(8,128)S(1)} %collective-permute-done.2.first_ref, f32[24,128]{1,0:T(8,128)S(1)} %collective-permute-done.side_ref, f32[8,128]{1,0:T(8,128)S(1)} %collective-permute-done.1.corner_ref, ...), custom_call_target="tpu_custom_call" | custom-call | bytes 1048576 | tf_op jit(solution)/shard_map/strain/strain/pallas_call | solution.py:51
  14.6 19.1 %all_to_all.10 = f32[64,1,896]{2,1,0:T(1,128)S(1)} all-to-all(f32[64,1,896]{2,1,0:T(1,128)S(1)} %bitcast.32), channel_id=1, replica_groups=mesh['gx'=8,'gy'=8,'gz'=4] {'gx','gy'}, dimensions={0} | all-to-all | bytes 458752 | tf_op jit(solution)/shard_map/exchange/all_to_all | solution.py:46
  33.6 3.9 %respond.1 = f32[384,128]{1,0:T(8,128)S(1)} custom-call(f32[448,128]{1,0:T(8,128)S(1)} %bitcast.31, f32[48,2048]{1,0:T(8,128)S(1)} %early_tangent.1.early_ref, f32[48,2048]{1,0:T(8,128)S(1)} %late_tangent.1.late_ref), custom_call_target="tpu_custom_call" | custom-call | bytes 1048576 | tf_op jit(solution)/shard_map/respond/respond/pallas_call | solution.py:51
  37.5 16.4 %all_to_all.11 = f32[64,1,768]{2,1,0:T(1,128)S(1)} all-to-all(f32[64,1,768]{2,1,0:T(1,128)S(1)} %bitcast.33), channel_id=1, replica_groups=mesh['gx'=8,'gy'=8,'gz'=4] {'gx','gy'}, dimensions={0} | all-to-all | bytes 393216 | tf_op jit(solution)/shard_map/return/all_to_all | solution.py:46
  53.9 1.1 %collect.1 = (f32[192,128]{1,0:T(8,128)S(1)}, f32[8,128]{1,0:T(8,128)S(1)}) custom-call(f32[384,128]{1,0:T(8,128)S(1)} %bitcast.34, s32[32,128]{1,0:T(8,128)S(1)} %get-tuple-element.30.helper_ref, f32[32,128]{1,0:T(8,128)S(1)} %get-tuple-element.48.rank_ref), custom_call_target="tpu_custom_call" | custom-call | bytes 1048576 | tf_op jit(solution)/shard_map/collect/collect/pallas_call | solution.py:51
  55.0 1.1 %collective-permute-start.5 = (f32[48,128]{1,0:T(8,128)S(1)}, f32[48,128]{1,0:T(8,128)S(1)}, u32[]{:S(2)}, u32[]{:S(2)}) collective-permute-start(f32[48,128]{1,0:T(8,128)S(1)} %slice_bitcast_fusion), channel_id=1, source_target_pairs={{0,32},{32,64},{64,96},{96,128},{128,160},{160,192},{192,224},{224... | collective-permute-start | bytes 73736 | tf_op jit(solution)/shard_map/settle/ppermute | solution.py:28
  56.1 2.3 %collective-permute-start.4 = (f32[8,128]{1,0:T(8,128)S(1)}, f32[8,128]{1,0:T(8,128)S(1)}, u32[]{:S(2)}, u32[]{:S(2)}) collective-permute-start(f32[8,128]{1,0:T(8,128)S(1)} %get-tuple-element.50), channel_id=1, source_target_pairs={{0,1},{1,2},{2,3},{3,0},{4,5},{5,6},{6,7},{7,4},{8,9},{9,10},{10,1... | collective-permute-start | bytes 12296 | tf_op jit(solution)/shard_map/settle/ppermute | solution.py:28
  58.4 1.3 %collective-permute-start.6 = (f32[8,128]{1,0:T(8,128)S(1)}, f32[8,128]{1,0:T(8,128)S(1)}, u32[]{:S(2)}, u32[]{:S(2)}) collective-permute-start(f32[8,128]{1,0:T(8,128)S(1)} %get-tuple-element.50), channel_id=1, source_target_pairs={{0,33},{1,34},{2,35},{32,65},{33,66},{34,67},{64,97},{65,98},{66,9... | collective-permute-start | bytes 12296 | tf_op jit(solution)/shard_map/settle/ppermute | solution.py:41
  59.8 0.0 collective-permute-done.4.last_ref
  59.8 5.1 %collective-permute-done.6.corner_ref = f32[8,128]{1,0:T(8,128)S(1)} collective-permute-done((f32[8,128]{1,0:T(8,128)S(1)}, f32[8,128]{1,0:T(8,128)S(1)}, u32[]{:S(2)}, u32[]{:S(2)}) %collective-permute-start.6) | collective-permute-done | bytes 4128 | tf_op jit(solution)/shard_map/settle/ppermute | solution.py:41
  64.8 0.0 collective-permute-done.5.side_ref
  64.9 1.9 %collective-permute-start.7 = (f32[34,128]{1,0:T(8,128)S(1)}, f32[34,128]{1,0:T(8,128)S(1)}, u32[]{:S(2)}, u32[]{:S(2)}) collective-permute-start(f32[34,128]{1,0:T(8,128)S(1)} %pad_maximum_fusion), channel_id=1, source_target_pairs={{0,4},{4,8},{8,12},{12,16},{16,20},{20,24},{24,28},{1,5},{5,9},{9,... | collective-permute-start | bytes 52232 | tf_op jit(solution)/shard_map/settle/ppermute | solution.py:41
  66.8 3.2 %collective-permute-done.7.prior_ref = f32[34,128]{1,0:T(8,128)S(1)} collective-permute-done((f32[34,128]{1,0:T(8,128)S(1)}, f32[34,128]{1,0:T(8,128)S(1)}, u32[]{:S(2)}, u32[]{:S(2)}) %collective-permute-start.7) | collective-permute-done | bytes 17440 | tf_op jit(solution)/shard_map/settle/ppermute | solution.py:41
  70.0 1.4 %force.1 = f32[96,128]{1,0:T(8,128)} custom-call(s32[6]{0:T(128)S(1)} %convert_element_type.3.inside_ref, f32[192,128]{1,0:T(8,128)S(1)} %get-tuple-element.49.sens_ref, f32[8,128]{1,0:T(8,128)S(1)} %collective-permute-done.4.last_ref, f32[48,128]{1,0:T(8,128)S(1)} %collective-permute-done.5.side_ref, f32[8,128]{1,0:T(8,128)S(1)} %collective-permute-done.6.corner_ref, ...), custom_call_target="tpu_custom_call" | custom-call | bytes 1048576 | tf_op jit(solution)/shard_map/settle/force/pallas_call | solution.py:51
  (14 shorter events, 0.1 us)
Async XLA Ops:
  0.9 9.5 %collective-permute-start.1 = (f32[8,128]{1,0:T(8,128)S(1)}, f32[8,128]{1,0:T(8,128)S(1)}, u32[]{:S(2)}, u32[]{:S(2)}) collective-permute-start(f32[8,128]{1,0:T(8,128)S(1)} %get-tuple-element.29), channel_id=1, source_target_pairs={{0,227},{1,224},{2,225},{3,226},{32,3},{33,0},{34,1},{35,2},{64,35... | collective-permute-start | bytes 12296 | tf_op jit(solution)/shard_map/lift/ppermute | solution.py:28
  1.4 9.0 %collective-permute-start.2 = (f32[8,128]{1,0:T(8,128)S(1)}, f32[8,128]{1,0:T(8,128)S(1)}, u32[]{:S(2)}, u32[]{:S(2)}) collective-permute-start(f32[8,128]{1,0:T(8,128)S(1)} %get-tuple-element.29), channel_id=1, source_target_pairs={{0,3},{1,0},{2,1},{3,2},{4,7},{5,4},{6,5},{7,6},{8,11},{9,8},{10,9... | collective-permute-start | bytes 12296 | tf_op jit(solution)/shard_map/lift/ppermute | solution.py:28
  1.9 8.5 %collective-permute-start = (f32[24,128]{1,0:T(8,128)S(1)}, f32[24,128]{1,0:T(8,128)S(1)}, u32[]{:S(2)}, u32[]{:S(2)}) collective-permute-start(f32[24,128]{1,0:T(8,128)S(1)} %slice_bitcast_fusion.1), channel_id=1, source_target_pairs={{0,224},{32,0},{64,32},{96,64},{128,96},{160,128},{192,160},{224,1... | collective-permute-start | bytes 36872 | tf_op jit(solution)/shard_map/lift/ppermute | solution.py:28
  10.5 2.2 %collective-permute-start.3 = (f32[17,128]{1,0:T(8,128)S(1)}, f32[17,128]{1,0:T(8,128)S(1)}, u32[]{:S(2)}, u32[]{:S(2)}) collective-permute-start(f32[17,128]{1,0:T(8,128)S(1)} %pad_maximum_fusion.1), channel_id=1, source_target_pairs={{0,28},{4,0},{8,4},{12,8},{16,12},{20,16},{24,20},{28,24},{1,29},{... | collective-permute-start | bytes 26120 | tf_op jit(solution)/shard_map/lift/ppermute | solution.py:28
  55.0 9.8 %collective-permute-start.5 = (f32[48,128]{1,0:T(8,128)S(1)}, f32[48,128]{1,0:T(8,128)S(1)}, u32[]{:S(2)}, u32[]{:S(2)}) collective-permute-start(f32[48,128]{1,0:T(8,128)S(1)} %slice_bitcast_fusion), channel_id=1, source_target_pairs={{0,32},{32,64},{64,96},{96,128},{128,160},{160,192},{192,224},{224... | collective-permute-start | bytes 73736 | tf_op jit(solution)/shard_map/settle/ppermute | solution.py:28
  56.1 3.6 %collective-permute-start.4 = (f32[8,128]{1,0:T(8,128)S(1)}, f32[8,128]{1,0:T(8,128)S(1)}, u32[]{:S(2)}, u32[]{:S(2)}) collective-permute-start(f32[8,128]{1,0:T(8,128)S(1)} %get-tuple-element.50), channel_id=1, source_target_pairs={{0,1},{1,2},{2,3},{3,0},{4,5},{5,6},{6,7},{7,4},{8,9},{9,10},{10,1... | collective-permute-start | bytes 12296 | tf_op jit(solution)/shard_map/settle/ppermute | solution.py:28
  58.4 6.4 %collective-permute-start.6 = (f32[8,128]{1,0:T(8,128)S(1)}, f32[8,128]{1,0:T(8,128)S(1)}, u32[]{:S(2)}, u32[]{:S(2)}) collective-permute-start(f32[8,128]{1,0:T(8,128)S(1)} %get-tuple-element.50), channel_id=1, source_target_pairs={{0,33},{1,34},{2,35},{32,65},{33,66},{34,67},{64,97},{65,98},{66,9... | collective-permute-start | bytes 12296 | tf_op jit(solution)/shard_map/settle/ppermute | solution.py:41
  64.9 5.1 %collective-permute-start.7 = (f32[34,128]{1,0:T(8,128)S(1)}, f32[34,128]{1,0:T(8,128)S(1)}, u32[]{:S(2)}, u32[]{:S(2)}) collective-permute-start(f32[34,128]{1,0:T(8,128)S(1)} %pad_maximum_fusion), channel_id=1, source_target_pairs={{0,4},{4,8},{8,12},{12,16},{16,20},{20,24},{24,28},{1,5},{5,9},{9,... | collective-permute-start | bytes 52232 | tf_op jit(solution)/shard_map/settle/ppermute | solution.py:41

commit v4 on v3

--- a/solution.py
+++ b/solution.py
@@ -140,8 +140,24 @@
         copy.wait()
 
 
+def last_lanes(block):
+    tile = transposed_lanes(block)[LANES - 8 :]
+    rows = block.shape[0]
+    return (tile + pltpu.roll(tile, rows, 1) + pltpu.roll(tile, 2 * rows, 1))[7:8]
+
+
 def route_kernel(
-    owners, helper_ref, weights_hbm, high_ref, low_ref, rank_ref, weights_ref, member_ref, ranks_ref, sem
+    owners,
+    helper_ref,
+    weights_hbm,
+    high_ref,
+    low_ref,
+    rank_ref,
+    edge_ref,
+    weights_ref,
+    member_ref,
+    ranks_ref,
+    sem,
 ):
     copy = pltpu.make_async_copy(weights_hbm.at[pl.ds(0, weights_ref.shape[0])], weights_ref, sem)
     copy.start()
@@ -176,6 +192,14 @@
     high_ref[...] = jnp.where(lows < 0, -1, found[:owners])
     for bucket in range(owners):
         low_ref[:, pl.ds(bucket * LANES, LANES)] = one_hot(lows[bucket : bucket + 1])
+    edge_ref[...] = jnp.concatenate(
+        [
+            last_lanes(helper_ref[...].astype(jnp.float32)),
+            last_lanes(rank_ref[...]),
+            jnp.zeros((6, LANES), jnp.float32),
+        ],
+        0,
+    )
     copy.wait()
 
 
@@ -366,7 +390,39 @@
             out_ref[pl.ds(6 * (sender + i), 6), :] = stacked(found)[0:6]
 
 
-def collect_kernel(returned_ref, helper_ref, rank_ref, sens_ref, last_ref):
+def faces_kernel(
+    width_x, returned_ref, helper_ref, rank_ref, edge_ref, side_ref, end_ref, last_ref
+):
+    blocks = helper_ref.shape[0]
+    table = fields_first(returned_ref, 6)
+    edge = edge_ref[0:2].astype(jnp.int32)
+    plane = list(range(blocks - 8, blocks))
+    for group in (plane[:4], plane[4:], list(range(7, blocks - 8, 8)) + [blocks]):
+        highs, lows = [], []
+        for b in group:
+            highs.append(spread(helper_ref[pl.ds(b, 1), :] if b < blocks else edge[0:1]))
+            lows.append(one_hot(rank_ref[pl.ds(b, 1), :] if b < blocks else edge_ref[1:2]))
+        values = looked_up(table, 6, highs, jnp.concatenate(lows, 1))
+        for b, found in zip(group, values):
+            for f in range(6):
+                row = found[f][0:1]
+                if b == blocks:
+                    continue
+                if b >= blocks - 8:
+                    side_ref[pl.ds(8 * f + b - blocks + 8, 1), :] = row
+                if b % 8 == 7:
+                    end_ref[pl.ds(width_x * f + b // 8, 1), :] = row
+            if b == blocks:
+                part = iota((8, LANES), 1) // blocks
+                for half in range(2):
+                    row = jnp.zeros((8, LANES), jnp.float32)
+                    for g in range(3):
+                        row = jnp.where(part == g, found[3 * half + g], row)
+                    last_ref[pl.ds(half, 1), :] = row[0:1]
+    last_ref[pl.ds(2, 6), :] = jnp.zeros((6, LANES), jnp.float32)
+
+
+def collect_kernel(returned_ref, helper_ref, rank_ref, sens_ref):
     blocks = helper_ref.shape[0]
     table = fields_first(returned_ref, 6)
     for block in range(0, blocks, STEP):
@@ -376,11 +432,6 @@
         for i, found in enumerate(looked_up(table, 6, highs, columns)):
             for f in range(6):
                 sens_ref[pl.ds(blocks * f + block + i, 1), :] = found[f][0:1]
-    half = 3 * blocks
-    for part in range(2):
-        turned = transposed_lanes(sens_ref[pl.ds(half * part, half), :])
-        last_ref[pl.ds(part, 1), :] = turned[LANES - 1 : LANES]
-    last_ref[pl.ds(2, 6), :] = jnp.zeros((6, LANES), jnp.float32)
 
 
 def force_kernel(width_x, inside_ref, sens_ref, last_ref, side_ref, corner_ref, prior_ref, out_ref):
@@ -391,8 +442,9 @@
     rows = jnp.concatenate(
         [
             last_ref[0:2],
+            side_ref[54:56],
             corner_ref[0:2],
-            prior_ref[30:34],
+            side_ref[56:58],
         ],
         0,
     )
@@ -407,7 +459,7 @@
                 spot, column = blocks * g + 8 * x, part
             else:
                 here = side_ref[pl.ds(8 * f, 8), :]
-                above = prior_ref[pl.ds(planes * fields + f, 1), :]
+                above = side_ref[pl.ds(8 * fields + f, 1), :]
                 spot, column = blocks * g + 8 * (planes - 1), part + 2
             edge = jnp.where(in_z, edges[spot : spot + 8, column : column + 1], 0.0)
             corner = jnp.where(in_z, edges[spot + 7 : spot + 8, column + 4 : column + 5], 0.0)
@@ -470,13 +522,14 @@
 
     with jax.named_scope("route"):
         weights_hbm = pltpu.with_memory_space_constraint(fibre_weights, pltpu.HBM)
-        high, low, rank, weights = whole_call(
+        high, low, rank, edge, weights = whole_call(
             functools.partial(route_kernel, owners),
             "route",
             [
                 i32(owners, LANES),
                 jax.ShapeDtypeStruct((LANES, owners * LANES), jnp.bfloat16),
                 f32(blocks, LANES),
+                f32(8, LANES),
                 jax.ShapeDtypeStruct((points // 2, fibres), fibre_weights.dtype),
             ],
             (helper, weights_hbm),
@@ -517,8 +570,8 @@
         side = passed_round(disp_grid[:, 0].reshape(24, LANES), ("gx",), -1)
         corner = passed_round(first, ("gx", "gz"), -1)
         first = passed_round(first, ("gz",), -1)
-        side, corner, first, high, low, rank, early, inside = lax.optimization_barrier(
-            (side, corner, first, high, low, rank, early, inside)
+        side, corner, first, high, low, rank, edge, early, inside = lax.optimization_barrier(
+            (side, corner, first, high, low, rank, edge, early, inside)
         )
         next_y = jnp.concatenate(
             [
@@ -562,28 +615,28 @@
         returned = exchanged(answer, owners, ("gx", "gy"))
 
     with jax.named_scope("collect"):
-        sens, last = whole_call(
+        side, end, last = whole_call(
+            functools.partial(faces_kernel, width_x),
+            "faces",
+            [f32(48, LANES), f32(6 * width_x, LANES), f32(8, LANES)],
+            (returned, helper, rank, edge),
+        )
+        sens = whole_call(
             collect_kernel,
             "collect",
-            [f32(6 * blocks, LANES), f32(8, LANES)],
+            f32(6 * blocks, LANES),
             (returned, helper, rank),
         )
 
     with jax.named_scope("settle"):
-        sens_grid = sens.reshape(6, width_x, width_y, LANES)
-        side = passed_round(sens_grid[:, -1].reshape(48, LANES), ("gx",), 1)
-        corner = passed_on(last, ("gx", "gz"), 1)
+        prior = passed_round(end, ("gy",), 1)
+        corner = passed_on(last, ("gy", "gz"), 1)
         last = passed_round(last, ("gz",), 1)
-        prior = jnp.concatenate(
-            [
-                sens_grid[:, :, -1].reshape(6 * width_x, LANES),
-                side[7:48:8],
-                last[0:2],
-                corner[0:2],
-            ],
-            0,
-        )
-        prior = passed_on(prior, ("gy",), 1)
+        side = jnp.concatenate(
+            [side, prior[width_x - 1 : 6 * width_x : width_x], last[0:2], corner[0:2]], 0
+        )
+        side = passed_on(side, ("gx",), 1)
+        side, sens = lax.optimization_barrier((side, sens))
         force = whole_call(
             functools.partial(force_kernel, width_x),
             "force",

time: 71.7 us -> 70.2 us (0.979)
  waiting for transfers between devices: 8.26 us -> 6.44 us
    ppermute x2, waiting for transfers between devices: 8.23 us -> 6.39 us  [passed_on(): return lax.ppermute(array, axes, pairs)]
    ppermute x2, starting transfers between devices: 3.2 us -> 4.13 us  [passed_on(): return lax.ppermute(array, axes, pairs)]
    ppermute x6, starting transfers between devices: 10.3 us -> 9.34 us  [passed_round(): return lax.ppermute(array, axes, pairs)]
    pallas_call x8 -> x9, Pallas kernels: 13.8 us -> 14.2 us  [whole_call(): pl.pallas_call(kernel, name=name, out_shape=out, in_specs=places or [VMEM...]
  transfers between devices with their start and end apart: 8 -> 8, of which waited for: 2 -> 2; matrix products, arithmetic and copies ran while one was open for 0% -> 0% of each run, Pallas kernels for 7% -> 8%
where the time goes in v4:
time: 70.2 us; the launch traced here: 69.9 us
  blocking collectives  35.5 us (51%)
  Pallas kernels  14.2 us (20%)
  starting transfers between devices  13.5 us (19%)
  waiting for transfers between devices  6.44 us (9%)
    all_to_all x2, blocking collectives, exchanged(): flat = lax.all_to_all(flat, axes, split_axis=0, concat_axis=0, tiled=True)  35.5 us
    pallas_call x9, Pallas kernels, whole_call(): pl.pallas_call(kernel, name=name, out_shape=out, in_specs=places or [VMEM...  14.2 us
    ppermute x6, starting transfers between devices, passed_round(): return lax.ppermute(array, axes, pairs)  9.34 us
    ppermute x2, waiting for transfers between devices, passed_on(): return lax.ppermute(array, axes, pairs)  6.39 us
    ppermute x2, starting transfers between devices, passed_on(): return lax.ppermute(array, axes, pairs)  4.13 us
  transfers between devices with their start and end apart: 8, of which 2 were waited for; matrix products, arithmetic and copies ran while one was open for 0% of the time, Pallas kernels for 8%

profile of v4, /device:TPU:46, one launch (start us, length us, event | category | flops | bytes accessed | tf_op | source)
XLA Modules:
  0.0 69.9 jit_solution(7562280765257005727)
XLA Ops:
  0.0 0.9 %fetch.1 = (f32[8,128]{1,0:T(8,128)S(1)}, f32[96,128]{1,0:T(8,128)S(1)}, s32[32,128]{1,0:T(8,128)S(1)}, s32[32,128]{1,0:T(8,128)S(1)}, s32[32,128]{1,0:T(8,128)S...) custom-call(f32[96,128]{1,0:T(8,128)} %bitcast.30, s32[32,128]{1,0:T(8,128)} %bitcast.32, s32[32,128]{1,0:T(8,128)} %bitcast.33, ...), custom_call_target="tpu_custom_call" | custom-call | bytes 1048576 | tf_op jit(solution)/shard_map/fetch/fetch/pallas_call | solution.py:51
  0.9 0.5 collective-permute-start.1
  1.4 0.5 collective-permute-start.2
  1.9 5.8 %collective-permute-start = (f32[24,128]{1,0:T(8,128)S(1)}, f32[24,128]{1,0:T(8,128)S(1)}, u32[]{:S(2)}, u32[]{:S(2)}) collective-permute-start(f32[24,128]{1,0:T(8,128)S(1)} %slice_bitcast_fusion), channel_id=1, source_target_pairs={{0,224},{32,0},{64,32},{96,64},{128,96},{160,128},{192,160},{224,1... | collective-permute-start | bytes 36872 | tf_op jit(solution)/shard_map/lift/ppermute | solution.py:28
  7.8 1.6 %route.1 = (s32[64,128]{1,0:T(8,128)S(1)}, bf16[128,8192]{1,0:T(8,128)(2,1)S(1)}, f32[32,128]{1,0:T(8,128)S(1)}, f32[8,128]{1,0:T(8,128)S(1)}, bf16[2048,512]{1,0:T(8,128)(2,1)S(1)}) custom-call(s32[32,128]{1,0:T(8,128)S(1)} %get-tuple-element.35.helper_ref, bf16[4096,512]{1,0:T(8,128)(2,1)} %weights_hbm.3), custom_call_target="tpu_custom_call" | custom-call | flops 134217728 | bytes 1048576 | tf_op jit(solution)/shard_map/route/route/pallas_call | solution.py:51
  9.4 0.8 %early_tangent.1.early_ref = f32[48,2048]{1,0:T(8,128)S(1)} custom-call(bf16[2048,512]{1,0:T(8,128)(2,1)S(1)} %get-tuple-element.40.weights_ref, s32[32,128]{1,0:T(8,128)S(1)} %get-tuple-element.41.class_ref, bf16[36,512]{1,0:T(8,128)(2,1)S(1)} %get-tuple-element.42.blocks_ref, f32[6,6]{1,0:T(8,128)S(1)} %get-tuple-element.43.matrix_ref), custom_call_target="tpu_custom_call" | custom-call | flops 536870912 | bytes 1048576 | tf_op jit(solution)/shard_map/tangent/early_tangent/pallas_call | solution.py:51
  10.3 0.1 stack.27
  10.4 0.0 collective-permute-done.1.corner_ref
  10.4 0.0 collective-permute-done.2.first_ref
  10.4 0.0 collective-permute-done.side_ref
  10.5 0.0 collective-permute-start.3
  10.5 2.2 %late_tangent.1.late_ref = f32[48,2048]{1,0:T(8,128)S(1)} custom-call(bf16[4096,512]{1,0:T(8,128)(2,1)} %weights_hbm.3, s32[32,128]{1,0:T(8,128)S(1)} %get-tuple-element.41.class_ref, bf16[36,512]{1,0:T(8,128)(2,1)S(1)} %get-tuple-element.42.blocks_ref, f32[6,6]{1,0:T(8,128)S(1)} %get-tuple-element.43.matrix_ref), custom_call_target="tpu_custom_call" | custom-call | flops 536870912 | bytes 1048576 | tf_op jit(solution)/shard_map/tangent/late_tangent/pallas_call | solution.py:51
  12.7 0.0 collective-permute-done.3.next_ref
  12.7 1.8 %strain.1 = f32[448,128]{1,0:T(8,128)S(1)} custom-call(s32[6]{0:T(128)S(1)} %convert_element_type.3.inside_ref, f32[96,128]{1,0:T(8,128)S(1)} %get-tuple-element.33.disp_ref, f32[8,128]{1,0:T(8,128)S(1)} %collective-permute-done.2.first_ref, f32[24,128]{1,0:T(8,128)S(1)} %collective-permute-done.side_ref, f32[8,128]{1,0:T(8,128)S(1)} %collective-permute-done.1.corner_ref, ...), custom_call_target="tpu_custom_call" | custom-call | bytes 1048576 | tf_op jit(solution)/shard_map/strain/strain/pallas_call | solution.py:51
  14.6 19.1 %all_to_all.10 = f32[64,1,896]{2,1,0:T(1,128)S(1)} all-to-all(f32[64,1,896]{2,1,0:T(1,128)S(1)} %bitcast.26), channel_id=1, replica_groups=mesh['gx'=8,'gy'=8,'gz'=4] {'gx','gy'}, dimensions={0} | all-to-all | bytes 458752 | tf_op jit(solution)/shard_map/exchange/all_to_all | solution.py:46
  33.6 3.9 %respond.1 = f32[384,128]{1,0:T(8,128)S(1)} custom-call(f32[448,128]{1,0:T(8,128)S(1)} %bitcast.25, f32[48,2048]{1,0:T(8,128)S(1)} %early_tangent.1.early_ref, f32[48,2048]{1,0:T(8,128)S(1)} %late_tangent.1.late_ref), custom_call_target="tpu_custom_call" | custom-call | bytes 1048576 | tf_op jit(solution)/shard_map/respond/respond/pallas_call | solution.py:51
  37.5 16.4 %all_to_all.11 = f32[64,1,768]{2,1,0:T(1,128)S(1)} all-to-all(f32[64,1,768]{2,1,0:T(1,128)S(1)} %bitcast.27), channel_id=1, replica_groups=mesh['gx'=8,'gy'=8,'gz'=4] {'gx','gy'}, dimensions={0} | all-to-all | bytes 393216 | tf_op jit(solution)/shard_map/return/all_to_all | solution.py:46
  53.9 0.5 faces.1
  54.4 0.2 collective-permute-start.4
  54.6 2.3 %collective-permute-start.5 = (f32[8,128]{1,0:T(8,128)S(1)}, f32[8,128]{1,0:T(8,128)S(1)}, u32[]{:S(2)}, u32[]{:S(2)}) collective-permute-start(f32[8,128]{1,0:T(8,128)S(1)} %get-tuple-element.58), channel_id=1, source_target_pairs={{0,1},{1,2},{2,3},{3,0},{4,5},{5,6},{6,7},{7,4},{8,9},{9,10},{10,1... | collective-permute-start | bytes 12296 | tf_op jit(solution)/shard_map/settle/ppermute | solution.py:28
  56.9 1.3 %collective-permute-start.6 = (f32[8,128]{1,0:T(8,128)S(1)}, f32[8,128]{1,0:T(8,128)S(1)}, u32[]{:S(2)}, u32[]{:S(2)}) collective-permute-start(f32[8,128]{1,0:T(8,128)S(1)} %get-tuple-element.58), channel_id=1, source_target_pairs={{0,5},{1,6},{2,7},{4,9},{5,10},{6,11},{8,13},{9,14},{10,15},{12,17... | collective-permute-start | bytes 12296 | tf_op jit(solution)/shard_map/settle/ppermute | solution.py:41
  58.2 0.0 collective-permute-done.5.last_ref
  58.2 4.5 %collective-permute-done.6.corner_ref = f32[8,128]{1,0:T(8,128)S(1)} collective-permute-done((f32[8,128]{1,0:T(8,128)S(1)}, f32[8,128]{1,0:T(8,128)S(1)}, u32[]{:S(2)}, u32[]{:S(2)}) %collective-permute-start.6) | collective-permute-done | bytes 4128 | tf_op jit(solution)/shard_map/settle/ppermute | solution.py:41
  62.7 0.0 collective-permute-done.4.prior_ref
  62.7 2.9 %collective-permute-start.7 = (f32[58,128]{1,0:T(8,128)S(1)}, f32[58,128]{1,0:T(8,128)S(1)}, u32[]{:S(2)}, u32[]{:S(2)}) collective-permute-start(f32[58,128]{1,0:T(8,128)S(1)} %pad_maximum_fusion), channel_id=1, source_target_pairs={{0,32},{32,64},{64,96},{96,128},{128,160},{160,192},{192,224},{1,3... | collective-permute-start | bytes 89096 | tf_op jit(solution)/shard_map/settle/ppermute | solution.py:41
  65.6 1.0 %collect.1.sens_ref = f32[192,128]{1,0:T(8,128)S(1)} custom-call(f32[384,128]{1,0:T(8,128)S(1)} %bitcast.24, s32[32,128]{1,0:T(8,128)S(1)} %get-tuple-element.35.helper_ref, f32[32,128]{1,0:T(8,128)S(1)} %get-tuple-element.54.rank_ref), custom_call_target="tpu_custom_call" | custom-call | bytes 1048576 | tf_op jit(solution)/shard_map/collect/collect/pallas_call | solution.py:51
  66.6 1.9 %collective-permute-done.7.side_ref = f32[58,128]{1,0:T(8,128)S(1)} collective-permute-done((f32[58,128]{1,0:T(8,128)S(1)}, f32[58,128]{1,0:T(8,128)S(1)}, u32[]{:S(2)}, u32[]{:S(2)}) %collective-permute-start.7) | collective-permute-done | bytes 29728 | tf_op jit(solution)/shard_map/settle/ppermute | solution.py:41
  68.5 1.4 %force.1 = f32[96,128]{1,0:T(8,128)} custom-call(s32[6]{0:T(128)S(1)} %convert_element_type.3.inside_ref, f32[192,128]{1,0:T(8,128)S(1)} %collect.1.sens_ref, f32[8,128]{1,0:T(8,128)S(1)} %collective-permute-done.5.last_ref, f32[58,128]{1,0:T(8,128)S(1)} %collective-permute-done.7.side_ref, f32[8,128]{1,0:T(8,128)S(1)} %collective-permute-done.6.corner_ref, ...), custom_call_target="tpu_custom_call" | custom-call | bytes 1048576 | tf_op jit(solution)/shard_map/settle/force/pallas_call | solution.py:51
  (12 shorter events, 0.1 us)
Async XLA Ops:
  0.9 9.5 %collective-permute-start.1 = (f32[8,128]{1,0:T(8,128)S(1)}, f32[8,128]{1,0:T(8,128)S(1)}, u32[]{:S(2)}, u32[]{:S(2)}) collective-permute-start(f32[8,128]{1,0:T(8,128)S(1)} %get-tuple-element.34), channel_id=1, source_target_pairs={{0,227},{1,224},{2,225},{3,226},{32,3},{33,0},{34,1},{35,2},{64,35... | collective-permute-start | bytes 12296 | tf_op jit(solution)/shard_map/lift/ppermute | solution.py:28
  1.4 9.0 %collective-permute-start.2 = (f32[8,128]{1,0:T(8,128)S(1)}, f32[8,128]{1,0:T(8,128)S(1)}, u32[]{:S(2)}, u32[]{:S(2)}) collective-permute-start(f32[8,128]{1,0:T(8,128)S(1)} %get-tuple-element.34), channel_id=1, source_target_pairs={{0,3},{1,0},{2,1},{3,2},{4,7},{5,4},{6,5},{7,6},{8,11},{9,8},{10,9... | collective-permute-start | bytes 12296 | tf_op jit(solution)/shard_map/lift/ppermute | solution.py:28
  1.9 8.5 %collective-permute-start = (f32[24,128]{1,0:T(8,128)S(1)}, f32[24,128]{1,0:T(8,128)S(1)}, u32[]{:S(2)}, u32[]{:S(2)}) collective-permute-start(f32[24,128]{1,0:T(8,128)S(1)} %slice_bitcast_fusion), channel_id=1, source_target_pairs={{0,224},{32,0},{64,32},{96,64},{128,96},{160,128},{192,160},{224,1... | collective-permute-start | bytes 36872 | tf_op jit(solution)/shard_map/lift/ppermute | solution.py:28
  10.5 2.2 %collective-permute-start.3 = (f32[17,128]{1,0:T(8,128)S(1)}, f32[17,128]{1,0:T(8,128)S(1)}, u32[]{:S(2)}, u32[]{:S(2)}) collective-permute-start(f32[17,128]{1,0:T(8,128)S(1)} %pad_maximum_fusion.1), channel_id=1, source_target_pairs={{0,28},{4,0},{8,4},{12,8},{16,12},{20,16},{24,20},{28,24},{1,29},{... | collective-permute-start | bytes 26120 | tf_op jit(solution)/shard_map/lift/ppermute | solution.py:28
  54.4 8.3 %collective-permute-start.4 = (f32[24,128]{1,0:T(8,128)S(1)}, f32[24,128]{1,0:T(8,128)S(1)}, u32[]{:S(2)}, u32[]{:S(2)}) collective-permute-start(f32[24,128]{1,0:T(8,128)S(1)} %get-tuple-element.57), channel_id=1, source_target_pairs={{0,4},{4,8},{8,12},{12,16},{16,20},{20,24},{24,28},{28,0},{1,5},{5... | collective-permute-start | bytes 36872 | tf_op jit(solution)/shard_map/settle/ppermute | solution.py:28
  54.6 3.6 %collective-permute-start.5 = (f32[8,128]{1,0:T(8,128)S(1)}, f32[8,128]{1,0:T(8,128)S(1)}, u32[]{:S(2)}, u32[]{:S(2)}) collective-permute-start(f32[8,128]{1,0:T(8,128)S(1)} %get-tuple-element.58), channel_id=1, source_target_pairs={{0,1},{1,2},{2,3},{3,0},{4,5},{5,6},{6,7},{7,4},{8,9},{9,10},{10,1... | collective-permute-start | bytes 12296 | tf_op jit(solution)/shard_map/settle/ppermute | solution.py:28
  56.9 5.8 %collective-permute-start.6 = (f32[8,128]{1,0:T(8,128)S(1)}, f32[8,128]{1,0:T(8,128)S(1)}, u32[]{:S(2)}, u32[]{:S(2)}) collective-permute-start(f32[8,128]{1,0:T(8,128)S(1)} %get-tuple-element.58), channel_id=1, source_target_pairs={{0,5},{1,6},{2,7},{4,9},{5,10},{6,11},{8,13},{9,14},{10,15},{12,17... | collective-permute-start | bytes 12296 | tf_op jit(solution)/shard_map/settle/ppermute | solution.py:41
  62.7 5.8 %collective-permute-start.7 = (f32[58,128]{1,0:T(8,128)S(1)}, f32[58,128]{1,0:T(8,128)S(1)}, u32[]{:S(2)}, u32[]{:S(2)}) collective-permute-start(f32[58,128]{1,0:T(8,128)S(1)} %pad_maximum_fusion), channel_id=1, source_target_pairs={{0,32},{32,64},{64,96},{96,128},{128,160},{160,192},{192,224},{1,3... | collective-permute-start | bytes 89096 | tf_op jit(solution)/shard_map/settle/ppermute | solution.py:41

commit v5 on v4

--- a/solution.py
+++ b/solution.py
@@ -506,11 +506,10 @@
             rve_helper.reshape(blocks, LANES),
             rve_slot.reshape(blocks, LANES),
             rve_class.reshape(blocks, LANES),
-            fibre_blocks,
             matrix_tangent,
         )
         kept = [jax.ShapeDtypeStruct(a.shape, a.dtype) for a in inputs]
-        first, disp, helper, slot, level, fibre, matrix = whole_call(
+        first, disp, helper, slot, level, matrix = whole_call(
             functools.partial(fetch_kernel, len(inputs)),
             "fetch",
             [f32(8, LANES)] + kept,
@@ -548,7 +547,7 @@
             functools.partial(tangent_kernel, 0),
             "early_tangent",
             f32(48, half),
-            (weights, level, fibre, matrix),
+            (weights, level, fibre_blocks, matrix),
             [pltpu.VMEM((8, LANES), jnp.float32)],
             flops=256 * points * fibres,
         )
@@ -556,7 +555,7 @@
             functools.partial(fetched_tangent_kernel, half),
             "late_tangent",
             f32(48, half),
-            (weights_hbm, level, fibre, matrix),
+            (weights_hbm, level, fibre_blocks, matrix),
             [
                 pltpu.VMEM((8, LANES), jnp.float32),
                 pltpu.VMEM((half, fibres), jnp.bfloat16),

time: 70.2 us -> 70.2 us (level)
  no operation moved by 1% of the time
where the time goes in v5:
time: 70.2 us; the launch traced here: 69.9 us
  blocking collectives  35.4 us (50%)
  Pallas kernels  14.2 us (20%)
  starting transfers between devices  13.5 us (19%)
  waiting for transfers between devices  6.45 us (9%)
    all_to_all x2, blocking collectives, exchanged(): flat = lax.all_to_all(flat, axes, split_axis=0, concat_axis=0, tiled=True)  35.4 us
    pallas_call x9, Pallas kernels, whole_call(): pl.pallas_call(kernel, name=name, out_shape=out, in_specs=places or [VMEM...  14.2 us
    ppermute x6, starting transfers between devices, passed_round(): return lax.ppermute(array, axes, pairs)  9.33 us
    ppermute x2, waiting for transfers between devices, passed_on(): return lax.ppermute(array, axes, pairs)  6.4 us
    ppermute x2, starting transfers between devices, passed_on(): return lax.ppermute(array, axes, pairs)  4.13 us
  transfers between devices with their start and end apart: 8, of which 2 were waited for; matrix products, arithmetic and copies ran while one was open for 0% of the time, Pallas kernels for 8%

profile of v5, /device:TPU:46, one launch (start us, length us, event | category | flops | bytes accessed | tf_op | source)
XLA Modules:
  0.0 69.9 jit_solution(14570862642779678754)
XLA Ops:
  0.0 0.9 %fetch.1 = (f32[8,128]{1,0:T(8,128)S(1)}, f32[96,128]{1,0:T(8,128)S(1)}, s32[32,128]{1,0:T(8,128)S(1)}, s32[32,128]{1,0:T(8,128)S(1)}, s32[32,128]{1,0:T(8,128)S(1)}, /*index=5*/f32[6,6]{1,0:T(8,128)S(1)}) custom-call(f32[96,128]{1,0:T(8,128)} %bitcast.30, s32[32,128]{1,0:T(8,128)} %bitcast.32, s32[32,128]{1,0:T(8,128)} %bitcast.33, s32[32,128]{1,0:T(8,128)} %bitcast.34, ...), custom_call_target="tpu_custom_call" | custom-call | bytes 1048576 | tf_op jit(solution)/shard_map/fetch/fetch/pallas_call | solution.py:51
  0.9 0.5 collective-permute-start.1
  1.4 0.5 collective-permute-start.2
  1.9 5.8 %collective-permute-start = (f32[24,128]{1,0:T(8,128)S(1)}, f32[24,128]{1,0:T(8,128)S(1)}, u32[]{:S(2)}, u32[]{:S(2)}) collective-permute-start(f32[24,128]{1,0:T(8,128)S(1)} %slice_bitcast_fusion), channel_id=1, source_target_pairs={{0,224},{32,0},{64,32},{96,64},{128,96},{160,128},{192,160},{224,1... | collective-permute-start | bytes 36872 | tf_op jit(solution)/shard_map/lift/ppermute | solution.py:28
  7.8 0.0 copy-start
  7.8 1.6 %route.1 = (s32[64,128]{1,0:T(8,128)S(1)}, bf16[128,8192]{1,0:T(8,128)(2,1)S(1)}, f32[32,128]{1,0:T(8,128)S(1)}, f32[8,128]{1,0:T(8,128)S(1)}, bf16[2048,512]{1,0:T(8,128)(2,1)S(1)}) custom-call(s32[32,128]{1,0:T(8,128)S(1)} %get-tuple-element.34.helper_ref, bf16[4096,512]{1,0:T(8,128)(2,1)} %weights_hbm.3), custom_call_target="tpu_custom_call" | custom-call | flops 134217728 | bytes 1048576 | tf_op jit(solution)/shard_map/route/route/pallas_call | solution.py:51
  9.4 0.0 copy-done
  9.4 0.8 %early_tangent.1.early_ref = f32[48,2048]{1,0:T(8,128)S(1)} custom-call(bf16[2048,512]{1,0:T(8,128)(2,1)S(1)} %get-tuple-element.39.weights_ref, s32[32,128]{1,0:T(8,128)S(1)} %get-tuple-element.40.class_ref, bf16[36,512]{1,0:T(8,128)(2,1)S(1)} %copy-done, f32[6,6]{1,0:T(8,128)S(1)} %get-tuple-element.41.matrix_ref), custom_call_target="tpu_custom_call" | custom-call | flops 536870912 | bytes 1048576 | tf_op jit(solution)/shard_map/tangent/early_tangent/pallas_call | solution.py:51
  10.3 0.1 stack.27
  10.4 0.0 collective-permute-done.1.corner_ref
  10.4 0.0 collective-permute-done.2.first_ref
  10.4 0.0 collective-permute-done.side_ref
  10.5 0.0 collective-permute-start.3
  10.5 2.2 %late_tangent.1.late_ref = f32[48,2048]{1,0:T(8,128)S(1)} custom-call(bf16[4096,512]{1,0:T(8,128)(2,1)} %weights_hbm.3, s32[32,128]{1,0:T(8,128)S(1)} %get-tuple-element.40.class_ref, bf16[36,512]{1,0:T(8,128)(2,1)S(1)} %copy-done, f32[6,6]{1,0:T(8,128)S(1)} %get-tuple-element.41.matrix_ref), custom_call_target="tpu_custom_call" | custom-call | flops 536870912 | bytes 1048576 | tf_op jit(solution)/shard_map/tangent/late_tangent/pallas_call | solution.py:51
  12.7 0.0 collective-permute-done.3.next_ref
  12.7 1.8 %strain.1 = f32[448,128]{1,0:T(8,128)S(1)} custom-call(s32[6]{0:T(128)S(1)} %convert_element_type.3.inside_ref, f32[96,128]{1,0:T(8,128)S(1)} %get-tuple-element.32.disp_ref, f32[8,128]{1,0:T(8,128)S(1)} %collective-permute-done.2.first_ref, f32[24,128]{1,0:T(8,128)S(1)} %collective-permute-done.side_ref, f32[8,128]{1,0:T(8,128)S(1)} %collective-permute-done.1.corner_ref, ...), custom_call_target="tpu_custom_call" | custom-call | bytes 1048576 | tf_op jit(solution)/shard_map/strain/strain/pallas_call | solution.py:51
  14.6 19.1 %all_to_all.10 = f32[64,1,896]{2,1,0:T(1,128)S(1)} all-to-all(f32[64,1,896]{2,1,0:T(1,128)S(1)} %bitcast.26), channel_id=1, replica_groups=mesh['gx'=8,'gy'=8,'gz'=4] {'gx','gy'}, dimensions={0} | all-to-all | bytes 458752 | tf_op jit(solution)/shard_map/exchange/all_to_all | solution.py:46
  33.6 3.9 %respond.1 = f32[384,128]{1,0:T(8,128)S(1)} custom-call(f32[448,128]{1,0:T(8,128)S(1)} %bitcast.25, f32[48,2048]{1,0:T(8,128)S(1)} %early_tangent.1.early_ref, f32[48,2048]{1,0:T(8,128)S(1)} %late_tangent.1.late_ref), custom_call_target="tpu_custom_call" | custom-call | bytes 1048576 | tf_op jit(solution)/shard_map/respond/respond/pallas_call | solution.py:51
  37.5 16.4 %all_to_all.11 = f32[64,1,768]{2,1,0:T(1,128)S(1)} all-to-all(f32[64,1,768]{2,1,0:T(1,128)S(1)} %bitcast.27), channel_id=1, replica_groups=mesh['gx'=8,'gy'=8,'gz'=4] {'gx','gy'}, dimensions={0} | all-to-all | bytes 393216 | tf_op jit(solution)/shard_map/return/all_to_all | solution.py:46
  53.9 0.5 faces.1
  54.4 0.2 collective-permute-start.4
  54.6 2.3 %collective-permute-start.5 = (f32[8,128]{1,0:T(8,128)S(1)}, f32[8,128]{1,0:T(8,128)S(1)}, u32[]{:S(2)}, u32[]{:S(2)}) collective-permute-start(f32[8,128]{1,0:T(8,128)S(1)} %get-tuple-element.56), channel_id=1, source_target_pairs={{0,1},{1,2},{2,3},{3,0},{4,5},{5,6},{6,7},{7,4},{8,9},{9,10},{10,1... | collective-permute-start | bytes 12296 | tf_op jit(solution)/shard_map/settle/ppermute | solution.py:28
  56.9 1.3 %collective-permute-start.6 = (f32[8,128]{1,0:T(8,128)S(1)}, f32[8,128]{1,0:T(8,128)S(1)}, u32[]{:S(2)}, u32[]{:S(2)}) collective-permute-start(f32[8,128]{1,0:T(8,128)S(1)} %get-tuple-element.56), channel_id=1, source_target_pairs={{0,5},{1,6},{2,7},{4,9},{5,10},{6,11},{8,13},{9,14},{10,15},{12,17... | collective-permute-start | bytes 12296 | tf_op jit(solution)/shard_map/settle/ppermute | solution.py:41
  58.1 0.0 collective-permute-done.5.last_ref
  58.2 4.5 %collective-permute-done.6.corner_ref = f32[8,128]{1,0:T(8,128)S(1)} collective-permute-done((f32[8,128]{1,0:T(8,128)S(1)}, f32[8,128]{1,0:T(8,128)S(1)}, u32[]{:S(2)}, u32[]{:S(2)}) %collective-permute-start.6) | collective-permute-done | bytes 4128 | tf_op jit(solution)/shard_map/settle/ppermute | solution.py:41
  62.7 0.0 collective-permute-done.4.prior_ref
  62.7 2.9 %collective-permute-start.7 = (f32[58,128]{1,0:T(8,128)S(1)}, f32[58,128]{1,0:T(8,128)S(1)}, u32[]{:S(2)}, u32[]{:S(2)}) collective-permute-start(f32[58,128]{1,0:T(8,128)S(1)} %pad_maximum_fusion), channel_id=1, source_target_pairs={{0,32},{32,64},{64,96},{96,128},{128,160},{160,192},{192,224},{1,3... | collective-permute-start | bytes 89096 | tf_op jit(solution)/shard_map/settle/ppermute | solution.py:41
  65.6 1.0 %collect.1.sens_ref = f32[192,128]{1,0:T(8,128)S(1)} custom-call(f32[384,128]{1,0:T(8,128)S(1)} %bitcast.24, s32[32,128]{1,0:T(8,128)S(1)} %get-tuple-element.34.helper_ref, f32[32,128]{1,0:T(8,128)S(1)} %get-tuple-element.52.rank_ref), custom_call_target="tpu_custom_call" | custom-call | bytes 1048576 | tf_op jit(solution)/shard_map/collect/collect/pallas_call | solution.py:51
  66.6 1.9 %collective-permute-done.7.side_ref = f32[58,128]{1,0:T(8,128)S(1)} collective-permute-done((f32[58,128]{1,0:T(8,128)S(1)}, f32[58,128]{1,0:T(8,128)S(1)}, u32[]{:S(2)}, u32[]{:S(2)}) %collective-permute-start.7) | collective-permute-done | bytes 29728 | tf_op jit(solution)/shard_map/settle/ppermute | solution.py:41
  68.5 1.4 %force.1 = f32[96,128]{1,0:T(8,128)} custom-call(s32[6]{0:T(128)S(1)} %convert_element_type.3.inside_ref, f32[192,128]{1,0:T(8,128)S(1)} %collect.1.sens_ref, f32[8,128]{1,0:T(8,128)S(1)} %collective-permute-done.5.last_ref, f32[58,128]{1,0:T(8,128)S(1)} %collective-permute-done.7.side_ref, f32[8,128]{1,0:T(8,128)S(1)} %collective-permute-done.6.corner_ref, ...), custom_call_target="tpu_custom_call" | custom-call | bytes 1048576 | tf_op jit(solution)/shard_map/settle/force/pallas_call | solution.py:51
  (12 shorter events, 0.1 us)
Async XLA Ops:
  0.9 9.5 %collective-permute-start.1 = (f32[8,128]{1,0:T(8,128)S(1)}, f32[8,128]{1,0:T(8,128)S(1)}, u32[]{:S(2)}, u32[]{:S(2)}) collective-permute-start(f32[8,128]{1,0:T(8,128)S(1)} %get-tuple-element.33), channel_id=1, source_target_pairs={{0,227},{1,224},{2,225},{3,226},{32,3},{33,0},{34,1},{35,2},{64,35... | collective-permute-start | bytes 12296 | tf_op jit(solution)/shard_map/lift/ppermute | solution.py:28
  1.4 9.0 %collective-permute-start.2 = (f32[8,128]{1,0:T(8,128)S(1)}, f32[8,128]{1,0:T(8,128)S(1)}, u32[]{:S(2)}, u32[]{:S(2)}) collective-permute-start(f32[8,128]{1,0:T(8,128)S(1)} %get-tuple-element.33), channel_id=1, source_target_pairs={{0,3},{1,0},{2,1},{3,2},{4,7},{5,4},{6,5},{7,6},{8,11},{9,8},{10,9... | collective-permute-start | bytes 12296 | tf_op jit(solution)/shard_map/lift/ppermute | solution.py:28
  1.9 8.5 %collective-permute-start = (f32[24,128]{1,0:T(8,128)S(1)}, f32[24,128]{1,0:T(8,128)S(1)}, u32[]{:S(2)}, u32[]{:S(2)}) collective-permute-start(f32[24,128]{1,0:T(8,128)S(1)} %slice_bitcast_fusion), channel_id=1, source_target_pairs={{0,224},{32,0},{64,32},{96,64},{128,96},{160,128},{192,160},{224,1... | collective-permute-start | bytes 36872 | tf_op jit(solution)/shard_map/lift/ppermute | solution.py:28
  7.8 1.6 %copy-start = (bf16[36,512]{1,0:T(8,128)(2,1)S(1)}, bf16[36,512]{1,0:T(8,128)(2,1)}, u32[]{:S(2)}) copy-start(bf16[36,512]{1,0:T(8,128)(2,1)} %blocks_ref.3) | copy-start | bytes 110596
  10.5 2.2 %collective-permute-start.3 = (f32[17,128]{1,0:T(8,128)S(1)}, f32[17,128]{1,0:T(8,128)S(1)}, u32[]{:S(2)}, u32[]{:S(2)}) collective-permute-start(f32[17,128]{1,0:T(8,128)S(1)} %pad_maximum_fusion.1), channel_id=1, source_target_pairs={{0,28},{4,0},{8,4},{12,8},{16,12},{20,16},{24,20},{28,24},{1,29},{... | collective-permute-start | bytes 26120 | tf_op jit(solution)/shard_map/lift/ppermute | solution.py:28
  54.4 8.3 %collective-permute-start.4 = (f32[24,128]{1,0:T(8,128)S(1)}, f32[24,128]{1,0:T(8,128)S(1)}, u32[]{:S(2)}, u32[]{:S(2)}) collective-permute-start(f32[24,128]{1,0:T(8,128)S(1)} %get-tuple-element.55), channel_id=1, source_target_pairs={{0,4},{4,8},{8,12},{12,16},{16,20},{20,24},{24,28},{28,0},{1,5},{5... | collective-permute-start | bytes 36872 | tf_op jit(solution)/shard_map/settle/ppermute | solution.py:28
  54.6 3.6 %collective-permute-start.5 = (f32[8,128]{1,0:T(8,128)S(1)}, f32[8,128]{1,0:T(8,128)S(1)}, u32[]{:S(2)}, u32[]{:S(2)}) collective-permute-start(f32[8,128]{1,0:T(8,128)S(1)} %get-tuple-element.56), channel_id=1, source_target_pairs={{0,1},{1,2},{2,3},{3,0},{4,5},{5,6},{6,7},{7,4},{8,9},{9,10},{10,1... | collective-permute-start | bytes 12296 | tf_op jit(solution)/shard_map/settle/ppermute | solution.py:28
  56.9 5.8 %collective-permute-start.6 = (f32[8,128]{1,0:T(8,128)S(1)}, f32[8,128]{1,0:T(8,128)S(1)}, u32[]{:S(2)}, u32[]{:S(2)}) collective-permute-start(f32[8,128]{1,0:T(8,128)S(1)} %get-tuple-element.56), channel_id=1, source_target_pairs={{0,5},{1,6},{2,7},{4,9},{5,10},{6,11},{8,13},{9,14},{10,15},{12,17... | collective-permute-start | bytes 12296 | tf_op jit(solution)/shard_map/settle/ppermute | solution.py:41
  62.7 5.8 %collective-permute-start.7 = (f32[58,128]{1,0:T(8,128)S(1)}, f32[58,128]{1,0:T(8,128)S(1)}, u32[]{:S(2)}, u32[]{:S(2)}) collective-permute-start(f32[58,128]{1,0:T(8,128)S(1)} %pad_maximum_fusion), channel_id=1, source_target_pairs={{0,32},{32,64},{64,96},{96,128},{128,160},{160,192},{192,224},{1,3... | collective-permute-start | bytes 89096 | tf_op jit(solution)/shard_map/settle/ppermute | solution.py:41

commit v6 on v5

--- a/solution.py
+++ b/solution.py
@@ -383,11 +383,21 @@
             answer_ref[pl.ds(8 * b, 8), :] = total
 
     table = fields_first(answer_ref, 8)
-    for sender in range(0, owners, STEP):
-        columns = lows_ref[:, pl.ds(sender * LANES, STEP * LANES)]
-        highs = [spread(slot >> 7) for slot in slots[sender : sender + STEP]]
-        for i, found in enumerate(looked_up(table, 6, highs, columns)):
-            out_ref[pl.ds(6 * (sender + i), 6), :] = stacked(found)[0:6]
+    tiles = [answer_ref[pl.ds(8 * b, 8), :] for b in range(blocks)]
+    for sender in range(0, owners, STEP + 1):
+        steps = range(sender, min(sender + STEP, owners))
+        columns = lows_ref[:, pl.ds(sender * LANES, len(steps) * LANES)]
+        highs = [spread(slots[s] >> 7) for s in steps]
+        for s, found in zip(steps, looked_up(table, 6, highs, columns)):
+            out_ref[pl.ds(6 * s, 6), :] = stacked(found)[0:6]
+        if sender + STEP < owners:
+            s = sender + STEP
+            high, low = spread(slots[s] >> 7), spread(slots[s] & (LANES - 1))
+            total = jnp.zeros((8, LANES), jnp.float32)
+            for b, tile in enumerate(tiles):
+                taken = jnp.take_along_axis(tile, low, axis=1, mode="promise_in_bounds")
+                total = jnp.where(high == b, taken, total)
+            out_ref[pl.ds(6 * s, 6), :] = total[0:6]
 
 
 def faces_kernel(

time: 70.2 us -> 70.1 us (level)
  no operation moved by 1% of the time
where the time goes in v6:
time: 70.1 us; the launch traced here: 69.8 us
  blocking collectives  35.4 us (50%)
  Pallas kernels  14.1 us (20%)
  starting transfers between devices  13.5 us (19%)
  waiting for transfers between devices  6.44 us (9%)
    all_to_all x2, blocking collectives, exchanged(): flat = lax.all_to_all(flat, axes, split_axis=0, concat_axis=0, tiled=True)  35.4 us
    pallas_call x9, Pallas kernels, whole_call(): pl.pallas_call(kernel, name=name, out_shape=out, in_specs=places or [VMEM...  14.1 us
    ppermute x6, starting transfers between devices, passed_round(): return lax.ppermute(array, axes, pairs)  9.33 us
    ppermute x2, waiting for transfers between devices, passed_on(): return lax.ppermute(array, axes, pairs)  6.39 us
    ppermute x2, starting transfers between devices, passed_on(): return lax.ppermute(array, axes, pairs)  4.13 us
  transfers between devices with their start and end apart: 8, of which 2 were waited for; matrix products, arithmetic and copies ran while one was open for 0% of the time, Pallas kernels for 8%

profile of v6, /device:TPU:46, one launch (start us, length us, event | category | flops | bytes accessed | tf_op | source)
XLA Modules:
  0.0 69.8 jit_solution(12959406540212206052)
XLA Ops:
  0.0 0.9 %fetch.1 = (f32[8,128]{1,0:T(8,128)S(1)}, f32[96,128]{1,0:T(8,128)S(1)}, s32[32,128]{1,0:T(8,128)S(1)}, s32[32,128]{1,0:T(8,128)S(1)}, s32[32,128]{1,0:T(8,128)S(1)}, /*index=5*/f32[6,6]{1,0:T(8,128)S(1)}) custom-call(f32[96,128]{1,0:T(8,128)} %bitcast.30, s32[32,128]{1,0:T(8,128)} %bitcast.32, s32[32,128]{1,0:T(8,128)} %bitcast.33, s32[32,128]{1,0:T(8,128)} %bitcast.34, ...), custom_call_target="tpu_custom_call" | custom-call | bytes 1048576 | tf_op jit(solution)/shard_map/fetch/fetch/pallas_call | solution.py:51
  0.9 0.5 collective-permute-start.1
  1.4 0.5 collective-permute-start.2
  1.9 5.8 %collective-permute-start = (f32[24,128]{1,0:T(8,128)S(1)}, f32[24,128]{1,0:T(8,128)S(1)}, u32[]{:S(2)}, u32[]{:S(2)}) collective-permute-start(f32[24,128]{1,0:T(8,128)S(1)} %slice_bitcast_fusion), channel_id=1, source_target_pairs={{0,224},{32,0},{64,32},{96,64},{128,96},{160,128},{192,160},{224,1... | collective-permute-start | bytes 36872 | tf_op jit(solution)/shard_map/lift/ppermute | solution.py:28
  7.8 0.0 copy-start
  7.8 1.6 %route.1 = (s32[64,128]{1,0:T(8,128)S(1)}, bf16[128,8192]{1,0:T(8,128)(2,1)S(1)}, f32[32,128]{1,0:T(8,128)S(1)}, f32[8,128]{1,0:T(8,128)S(1)}, bf16[2048,512]{1,0:T(8,128)(2,1)S(1)}) custom-call(s32[32,128]{1,0:T(8,128)S(1)} %get-tuple-element.34.helper_ref, bf16[4096,512]{1,0:T(8,128)(2,1)} %weights_hbm.3), custom_call_target="tpu_custom_call" | custom-call | flops 134217728 | bytes 1048576 | tf_op jit(solution)/shard_map/route/route/pallas_call | solution.py:51
  9.4 0.0 copy-done
  9.4 0.8 %early_tangent.1.early_ref = f32[48,2048]{1,0:T(8,128)S(1)} custom-call(bf16[2048,512]{1,0:T(8,128)(2,1)S(1)} %get-tuple-element.39.weights_ref, s32[32,128]{1,0:T(8,128)S(1)} %get-tuple-element.40.class_ref, bf16[36,512]{1,0:T(8,128)(2,1)S(1)} %copy-done, f32[6,6]{1,0:T(8,128)S(1)} %get-tuple-element.41.matrix_ref), custom_call_target="tpu_custom_call" | custom-call | flops 536870912 | bytes 1048576 | tf_op jit(solution)/shard_map/tangent/early_tangent/pallas_call | solution.py:51
  10.3 0.1 stack.27
  10.4 0.0 collective-permute-done.1.corner_ref
  10.4 0.0 collective-permute-done.2.first_ref
  10.4 0.0 collective-permute-done.side_ref
  10.5 0.0 collective-permute-start.3
  10.5 2.2 %late_tangent.1.late_ref = f32[48,2048]{1,0:T(8,128)S(1)} custom-call(bf16[4096,512]{1,0:T(8,128)(2,1)} %weights_hbm.3, s32[32,128]{1,0:T(8,128)S(1)} %get-tuple-element.40.class_ref, bf16[36,512]{1,0:T(8,128)(2,1)S(1)} %copy-done, f32[6,6]{1,0:T(8,128)S(1)} %get-tuple-element.41.matrix_ref), custom_call_target="tpu_custom_call" | custom-call | flops 536870912 | bytes 1048576 | tf_op jit(solution)/shard_map/tangent/late_tangent/pallas_call | solution.py:51
  12.7 0.0 collective-permute-done.3.next_ref
  12.7 1.8 %strain.1 = f32[448,128]{1,0:T(8,128)S(1)} custom-call(s32[6]{0:T(128)S(1)} %convert_element_type.3.inside_ref, f32[96,128]{1,0:T(8,128)S(1)} %get-tuple-element.32.disp_ref, f32[8,128]{1,0:T(8,128)S(1)} %collective-permute-done.2.first_ref, f32[24,128]{1,0:T(8,128)S(1)} %collective-permute-done.side_ref, f32[8,128]{1,0:T(8,128)S(1)} %collective-permute-done.1.corner_ref, ...), custom_call_target="tpu_custom_call" | custom-call | bytes 1048576 | tf_op jit(solution)/shard_map/strain/strain/pallas_call | solution.py:51
  14.6 19.1 %all_to_all.10 = f32[64,1,896]{2,1,0:T(1,128)S(1)} all-to-all(f32[64,1,896]{2,1,0:T(1,128)S(1)} %bitcast.26), channel_id=1, replica_groups=mesh['gx'=8,'gy'=8,'gz'=4] {'gx','gy'}, dimensions={0} | all-to-all | bytes 458752 | tf_op jit(solution)/shard_map/exchange/all_to_all | solution.py:46
  33.6 3.7 %respond.1 = f32[384,128]{1,0:T(8,128)S(1)} custom-call(f32[448,128]{1,0:T(8,128)S(1)} %bitcast.25, f32[48,2048]{1,0:T(8,128)S(1)} %early_tangent.1.early_ref, f32[48,2048]{1,0:T(8,128)S(1)} %late_tangent.1.late_ref), custom_call_target="tpu_custom_call" | custom-call | bytes 1048576 | tf_op jit(solution)/shard_map/respond/respond/pallas_call | solution.py:51
  37.4 16.4 %all_to_all.11 = f32[64,1,768]{2,1,0:T(1,128)S(1)} all-to-all(f32[64,1,768]{2,1,0:T(1,128)S(1)} %bitcast.27), channel_id=1, replica_groups=mesh['gx'=8,'gy'=8,'gz'=4] {'gx','gy'}, dimensions={0} | all-to-all | bytes 393216 | tf_op jit(solution)/shard_map/return/all_to_all | solution.py:46
  53.8 0.5 faces.1
  54.3 0.2 collective-permute-start.4
  54.4 2.3 %collective-permute-start.5 = (f32[8,128]{1,0:T(8,128)S(1)}, f32[8,128]{1,0:T(8,128)S(1)}, u32[]{:S(2)}, u32[]{:S(2)}) collective-permute-start(f32[8,128]{1,0:T(8,128)S(1)} %get-tuple-element.56), channel_id=1, source_target_pairs={{0,1},{1,2},{2,3},{3,0},{4,5},{5,6},{6,7},{7,4},{8,9},{9,10},{10,1... | collective-permute-start | bytes 12296 | tf_op jit(solution)/shard_map/settle/ppermute | solution.py:28
  56.7 1.3 %collective-permute-start.6 = (f32[8,128]{1,0:T(8,128)S(1)}, f32[8,128]{1,0:T(8,128)S(1)}, u32[]{:S(2)}, u32[]{:S(2)}) collective-permute-start(f32[8,128]{1,0:T(8,128)S(1)} %get-tuple-element.56), channel_id=1, source_target_pairs={{0,5},{1,6},{2,7},{4,9},{5,10},{6,11},{8,13},{9,14},{10,15},{12,17... | collective-permute-start | bytes 12296 | tf_op jit(solution)/shard_map/settle/ppermute | solution.py:41
  58.0 0.0 collective-permute-done.5.last_ref
  58.1 4.5 %collective-permute-done.6.corner_ref = f32[8,128]{1,0:T(8,128)S(1)} collective-permute-done((f32[8,128]{1,0:T(8,128)S(1)}, f32[8,128]{1,0:T(8,128)S(1)}, u32[]{:S(2)}, u32[]{:S(2)}) %collective-permute-start.6) | collective-permute-done | bytes 4128 | tf_op jit(solution)/shard_map/settle/ppermute | solution.py:41
  62.5 0.0 collective-permute-done.4.prior_ref
  62.6 2.9 %collective-permute-start.7 = (f32[58,128]{1,0:T(8,128)S(1)}, f32[58,128]{1,0:T(8,128)S(1)}, u32[]{:S(2)}, u32[]{:S(2)}) collective-permute-start(f32[58,128]{1,0:T(8,128)S(1)} %pad_maximum_fusion), channel_id=1, source_target_pairs={{0,32},{32,64},{64,96},{96,128},{128,160},{160,192},{192,224},{1,3... | collective-permute-start | bytes 89096 | tf_op jit(solution)/shard_map/settle/ppermute | solution.py:41
  65.4 1.0 %collect.1.sens_ref = f32[192,128]{1,0:T(8,128)S(1)} custom-call(f32[384,128]{1,0:T(8,128)S(1)} %bitcast.24, s32[32,128]{1,0:T(8,128)S(1)} %get-tuple-element.34.helper_ref, f32[32,128]{1,0:T(8,128)S(1)} %get-tuple-element.52.rank_ref), custom_call_target="tpu_custom_call" | custom-call | bytes 1048576 | tf_op jit(solution)/shard_map/collect/collect/pallas_call | solution.py:51
  66.5 1.9 %collective-permute-done.7.side_ref = f32[58,128]{1,0:T(8,128)S(1)} collective-permute-done((f32[58,128]{1,0:T(8,128)S(1)}, f32[58,128]{1,0:T(8,128)S(1)}, u32[]{:S(2)}, u32[]{:S(2)}) %collective-permute-start.7) | collective-permute-done | bytes 29728 | tf_op jit(solution)/shard_map/settle/ppermute | solution.py:41
  68.4 1.4 %force.1 = f32[96,128]{1,0:T(8,128)} custom-call(s32[6]{0:T(128)S(1)} %convert_element_type.3.inside_ref, f32[192,128]{1,0:T(8,128)S(1)} %collect.1.sens_ref, f32[8,128]{1,0:T(8,128)S(1)} %collective-permute-done.5.last_ref, f32[58,128]{1,0:T(8,128)S(1)} %collective-permute-done.7.side_ref, f32[8,128]{1,0:T(8,128)S(1)} %collective-permute-done.6.corner_ref, ...), custom_call_target="tpu_custom_call" | custom-call | bytes 1048576 | tf_op jit(solution)/shard_map/settle/force/pallas_call | solution.py:51
  (12 shorter events, 0.1 us)
Async XLA Ops:
  0.9 9.5 %collective-permute-start.1 = (f32[8,128]{1,0:T(8,128)S(1)}, f32[8,128]{1,0:T(8,128)S(1)}, u32[]{:S(2)}, u32[]{:S(2)}) collective-permute-start(f32[8,128]{1,0:T(8,128)S(1)} %get-tuple-element.33), channel_id=1, source_target_pairs={{0,227},{1,224},{2,225},{3,226},{32,3},{33,0},{34,1},{35,2},{64,35... | collective-permute-start | bytes 12296 | tf_op jit(solution)/shard_map/lift/ppermute | solution.py:28
  1.4 9.0 %collective-permute-start.2 = (f32[8,128]{1,0:T(8,128)S(1)}, f32[8,128]{1,0:T(8,128)S(1)}, u32[]{:S(2)}, u32[]{:S(2)}) collective-permute-start(f32[8,128]{1,0:T(8,128)S(1)} %get-tuple-element.33), channel_id=1, source_target_pairs={{0,3},{1,0},{2,1},{3,2},{4,7},{5,4},{6,5},{7,6},{8,11},{9,8},{10,9... | collective-permute-start | bytes 12296 | tf_op jit(solution)/shard_map/lift/ppermute | solution.py:28
  1.9 8.5 %collective-permute-start = (f32[24,128]{1,0:T(8,128)S(1)}, f32[24,128]{1,0:T(8,128)S(1)}, u32[]{:S(2)}, u32[]{:S(2)}) collective-permute-start(f32[24,128]{1,0:T(8,128)S(1)} %slice_bitcast_fusion), channel_id=1, source_target_pairs={{0,224},{32,0},{64,32},{96,64},{128,96},{160,128},{192,160},{224,1... | collective-permute-start | bytes 36872 | tf_op jit(solution)/shard_map/lift/ppermute | solution.py:28
  7.8 1.6 %copy-start = (bf16[36,512]{1,0:T(8,128)(2,1)S(1)}, bf16[36,512]{1,0:T(8,128)(2,1)}, u32[]{:S(2)}) copy-start(bf16[36,512]{1,0:T(8,128)(2,1)} %blocks_ref.3) | copy-start | bytes 110596
  10.5 2.2 %collective-permute-start.3 = (f32[17,128]{1,0:T(8,128)S(1)}, f32[17,128]{1,0:T(8,128)S(1)}, u32[]{:S(2)}, u32[]{:S(2)}) collective-permute-start(f32[17,128]{1,0:T(8,128)S(1)} %pad_maximum_fusion.1), channel_id=1, source_target_pairs={{0,28},{4,0},{8,4},{12,8},{16,12},{20,16},{24,20},{28,24},{1,29},{... | collective-permute-start | bytes 26120 | tf_op jit(solution)/shard_map/lift/ppermute | solution.py:28
  54.3 8.3 %collective-permute-start.4 = (f32[24,128]{1,0:T(8,128)S(1)}, f32[24,128]{1,0:T(8,128)S(1)}, u32[]{:S(2)}, u32[]{:S(2)}) collective-permute-start(f32[24,128]{1,0:T(8,128)S(1)} %get-tuple-element.55), channel_id=1, source_target_pairs={{0,4},{4,8},{8,12},{12,16},{16,20},{20,24},{24,28},{28,0},{1,5},{5... | collective-permute-start | bytes 36872 | tf_op jit(solution)/shard_map/settle/ppermute | solution.py:28
  54.4 3.6 %collective-permute-start.5 = (f32[8,128]{1,0:T(8,128)S(1)}, f32[8,128]{1,0:T(8,128)S(1)}, u32[]{:S(2)}, u32[]{:S(2)}) collective-permute-start(f32[8,128]{1,0:T(8,128)S(1)} %get-tuple-element.56), channel_id=1, source_target_pairs={{0,1},{1,2},{2,3},{3,0},{4,5},{5,6},{6,7},{7,4},{8,9},{9,10},{10,1... | collective-permute-start | bytes 12296 | tf_op jit(solution)/shard_map/settle/ppermute | solution.py:28
  56.7 5.8 %collective-permute-start.6 = (f32[8,128]{1,0:T(8,128)S(1)}, f32[8,128]{1,0:T(8,128)S(1)}, u32[]{:S(2)}, u32[]{:S(2)}) collective-permute-start(f32[8,128]{1,0:T(8,128)S(1)} %get-tuple-element.56), channel_id=1, source_target_pairs={{0,5},{1,6},{2,7},{4,9},{5,10},{6,11},{8,13},{9,14},{10,15},{12,17... | collective-permute-start | bytes 12296 | tf_op jit(solution)/shard_map/settle/ppermute | solution.py:41
  62.6 5.8 %collective-permute-start.7 = (f32[58,128]{1,0:T(8,128)S(1)}, f32[58,128]{1,0:T(8,128)S(1)}, u32[]{:S(2)}, u32[]{:S(2)}) collective-permute-start(f32[58,128]{1,0:T(8,128)S(1)} %pad_maximum_fusion), channel_id=1, source_target_pairs={{0,32},{32,64},{64,96},{96,128},{128,160},{160,192},{192,224},{1,3... | collective-permute-start | bytes 89096 | tf_op jit(solution)/shard_map/settle/ppermute | solution.py:41
